TPU v7x, 32 devices: a whole 2x2x4 slice. The times are simulated.
32 devices in a mesh: node: 16 (over z, x, core), tp: 2 (over y).
Axes of the slice: x: 2, y: 2, z: 4, core: 2. Of those that a mesh axis runs over, the one named last changes fastest.
Arguments:
- query_rows: bfloat16 [4096, 8192], P('node', 'tp'), may hold values from -6 to 6
- key_rows: bfloat16 [4096, 1024], P('node', 'tp'), may hold values from -5 to 5
- value_rows: bfloat16 [4096, 1024], P('node', 'tp'), may hold values from -6 to 6
- out_weight: bfloat16 [8192, 4096], P('tp'), may hold values from -0.0625 to 0.0625
- out_grad: bfloat16 [4096, 4096], P(('node', 'tp')), may hold values from -6 to 6
- owner_slot: int32 [16], replicated, may hold values from 0 to 15, each once
Outputs:
- projected: bfloat16 [4096, 4096], P(('node', 'tp'))
- query_grad: bfloat16 [4096, 8192], P('node', 'tp')
- key_grad: bfloat16 [4096, 1024], P('node', 'tp')
- value_grad: bfloat16 [4096, 1024], P('node', 'tp')
Inputs may be any that keep to these rules, and one draw needn't show every extreme that they name: `owner_slot`: every slot holds exactly one tree node.
All inputs are finite; a program needn't handle non-finite values.
Results may differ from a plain program's by a relative error of at most 0.017.
Values may be sent and summed in bfloat16 or wider, within the bound.
No kernel may reach another device: no remote copies, remote signals or barrier semaphores. Data moves between devices by JAX's collectives and lax.ppermute only.
A program may use at most 256 MiB of HBM per device.

v0:
```python
import functools

import jax
import jax.numpy as jnp
from jax import lax
from jax.experimental import pallas as pl
from jax.experimental.pallas import tpu as pltpu
from jax.sharding import PartitionSpec as P

HEAD_DIM = 128
NODE_LEN = 256
CHAIN = 8
LEAVES = 8
PAIR = 2 * HEAD_DIM
COLUMNS = 512

masked_score = -1e30
score_scale = HEAD_DIM ** (-0.5)
log2_e = 1.4426950408889634


def dot(a, b):
    return jnp.dot(a, b, preferred_element_type=jnp.float32)


def dot_nt(a, b):
    return lax.dot_general(a, b, (((1,), (1,)), ((), ())), preferred_element_type=jnp.float32)


def attend(layout, owner_slot, *refs):
    piece_count, near_count, after_count, chunk_head, by_slot, old_count, head = layout
    q_any, own_any, weight_any = refs[:3]
    pieces, refs = refs[3 : 3 + piece_count], refs[3 + piece_count :]
    near, refs = refs[:near_count], refs[near_count:]
    old, rest = refs[:old_count], refs[old_count + after_count :]
    dq_any, proj_any, own_any_grad = rest[:3]
    parts = rest[3 : 4 if by_slot else 5]
    (
        far_ref, own_ref, out_grad, weight, proj, att, s_ref, p_ref, qs, ups, q_t, up_t,
        m_ref, l_ref, acc_ref, own_grad, slots, far_sem, slot_sem, q_sem, piece_sem, sem,
    ) = rest[3 + len(parts) :]
    me = lax.axis_index("node")
    node_count = owner_slot.shape[0]
    tree_node = jnp.int32(0)
    for n in range(node_count):
        tree_node = jnp.where(owner_slot[n] == me, n, tree_node)
    tree_nodes = CHAIN + LEAVES
    first_node = tree_node // tree_nodes * tree_nodes
    depth = jnp.minimum(tree_node - first_node, CHAIN)
    lineage = [owner_slot[first_node + b] for b in range(CHAIN)]

    def ancestor(b):
        return lineage[b] if isinstance(b, int) else owner_slot[first_node + b]

    rows = qs.shape[0]
    heads = rows // NODE_LEN
    half = HEAD_DIM
    width = heads * HEAD_DIM
    factor = score_scale * log2_e
    stride = slots.shape[0] // 4

    def head_rows(h):
        return pl.ds(h * NODE_LEN, NODE_LEN)

    def head_columns(h, first=0):
        return pl.ds(first + h * HEAD_DIM, HEAD_DIM)

    q_copies = [
        pltpu.make_async_copy(
            q_any.at[:, head_columns(h, head * width)], qs.at[head_rows(h), :], q_sem.at[h]
        )
        for h in range(heads)
    ]
    def pair_copies(source, target, sems):
        return [
            pltpu.make_async_copy(
                source.at[:, pl.ds(i * source.shape[1] // 2 + chunk_head * half, half)],
                target.at[:, pl.ds(i * half, half)],
                sems[i],
            )
            for i in range(2)
        ]

    own_copies = pair_copies(own_any, own_ref, [sem.at[0], sem.at[2]])
    weight_copy = pltpu.make_async_copy(
        weight_any.at[pl.ds(head * width, width), :], weight, sem.at[1]
    )
    order = lax.axis_index("tp") if piece_count == 2 else 0
    piece_rows = pieces[0].shape[0]
    piece_copies = [
        pltpu.make_async_copy(
            piece,
            out_grad.at[pl.ds(pl.multiple_of((order ^ i) * piece_rows, piece_rows), piece_rows), :],
            piece_sem.at[i],
        )
        for i, piece in enumerate(pieces)
    ]
    for copy in own_copies + q_copies:
        copy.start()

    def far_copies(source, index, b):
        return pair_copies(
            source.at[index], far_ref.at[b], [far_sem.at[b], far_sem.at[CHAIN + b]]
        )

    def fetch(b, carry):
        if near_count == 1:
            for copy in far_copies(near[0], ancestor(b), b):
                copy.start()
            return carry
        away = ancestor(b) ^ me
        for kind in range(near_count):

            @pl.when(away % 4 == kind)
            def _():
                for copy in far_copies(near[kind], away // 4, b):
                    copy.start()

        return carry

    lax.fori_loop(0, depth, fetch, 0)

    late_copies = [weight_copy] + piece_copies
    if head > 0:
        late_copies.append(pltpu.make_async_copy(old[1], proj, sem.at[3]))
    for copy in late_copies:
        copy.start()

    def fold_max(s):
        return jnp.maximum(s[:, :half], s[:, half:])

    for copy in own_copies + q_copies:
        copy.wait()
    s = dot_nt(qs[...], own_ref[:, :half])
    row = lax.broadcasted_iota(jnp.int32, (rows, NODE_LEN), 0) % NODE_LEN
    col = lax.broadcasted_iota(jnp.int32, (rows, NODE_LEN), 1)
    s = jnp.where(col <= row, s, masked_score)
    s_ref[CHAIN] = s
    m_ref[...] = fold_max(s)

    def score_block(b, carry):
        for copy in far_copies(near[0], 0, b):
            copy.wait()
        s = dot_nt(qs[...], far_ref[b, :, :half])
        s_ref[b] = s
        m_ref[...] = jnp.maximum(m_ref[...], fold_max(s))
        return carry

    lax.fori_loop(0, depth, score_block, 0)
    m_ref[...] = jnp.broadcast_to(jnp.max(m_ref[...], axis=1, keepdims=True), (rows, half))

    def weigh(b, values):
        top = m_ref[...]
        s = s_ref[b]
        p_low = jnp.exp2((s[:, :half] - top) * factor)
        p_high = jnp.exp2((s[:, half:] - top) * factor)
        p = jnp.concatenate([p_low, p_high], axis=1).astype(jnp.bfloat16)
        p_ref[b] = p
        return p_low + p_high, dot(p, values)

    part_sum, part = weigh(CHAIN, own_ref[:, half:])
    l_ref[...] = part_sum
    acc_ref[...] = part

    def forward_block(b, carry):
        part_sum, part = weigh(b, far_ref[b, :, half:])
        l_ref[...] += part_sum
        acc_ref[...] += part
        return carry

    lax.fori_loop(0, depth, forward_block, 0)
    inverse = 1.0 / jnp.broadcast_to(jnp.sum(l_ref[...], axis=1, keepdims=True), (rows, half))
    l_ref[...] = inverse
    attended = (acc_ref[...] * inverse).astype(jnp.bfloat16)
    for h in range(heads):
        att[:, head_columns(h)] = attended[h * NODE_LEN : (h + 1) * NODE_LEN, :]

    for copy in late_copies:
        copy.wait()
    for h in range(0, heads, 2):
        count = min(2, heads - h)
        two = dot_nt(out_grad[...], weight[h * HEAD_DIM : (h + count) * HEAD_DIM, :])
        for i in range(count):
            ups[head_rows(h + i), :] = two[:, i * HEAD_DIM : (i + 1) * HEAD_DIM].astype(jnp.bfloat16)

    def project(n, carry):
        columns = pl.ds(pl.multiple_of(n * COLUMNS, COLUMNS), COLUMNS)
        share = dot(att[...], weight[:, columns])
        proj[:, columns] = share if head == 0 else proj[:, columns] + share
        return carry

    lax.fori_loop(0, weight.shape[1] // COLUMNS, project, 0)
    proj_out = pltpu.make_async_copy(proj, proj_any, sem.at[4])
    proj_out.start()

    upstream = ups[...].astype(jnp.float32)
    corr_ref = m_ref
    corr_ref[...] = jnp.broadcast_to(
        jnp.sum(upstream * attended.astype(jnp.float32), axis=1, keepdims=True), (rows, half)
    )
    q_t[...] = (qs[...].astype(jnp.float32) * (inverse * score_scale)).astype(jnp.bfloat16).T
    up_t[...] = (upstream * inverse).astype(jnp.bfloat16).T

    def backward(b, keys, values):
        corr = corr_ref[...]
        p = p_ref[b]
        d_prob = dot_nt(ups[...], values)
        centred = jnp.concatenate([d_prob[:, :half] - corr, d_prob[:, half:] - corr], axis=1)
        d_score = (p.astype(jnp.float32) * centred).astype(jnp.bfloat16)
        grad = jnp.concatenate([dot(q_t[...], d_score), dot(up_t[...], p)], axis=0)
        return dot(d_score, keys), grad

    def slot_place(b):
        if by_slot:
            return ancestor(b)
        away = ancestor(b) ^ me
        kind = away % 4
        return away // 4 + stride * jnp.where(kind == 0, 0, jnp.where(kind == 2, 1, 2 + kind // 2))

    slots[...] = jnp.zeros_like(slots)
    part, grad = backward(CHAIN, own_ref[:, :half], own_ref[:, half:])
    acc_ref[...] = part
    own_grad[...] = grad.T
    own_out = pltpu.make_async_copy(own_grad, own_any_grad, sem.at[3])
    own_out.start()

    def backward_block(b, carry):
        part, grad = backward(b, far_ref[b, :, :half], far_ref[b, :, half:])
        acc_ref[...] += part
        block = grad.astype(jnp.bfloat16).T
        slots[slot_place(b)] = block
        return carry

    lax.fori_loop(0, depth, backward_block, 0)
    if by_slot:
        part_copies = [pltpu.make_async_copy(slots, parts[0].at[:, head], slot_sem.at[0])]
    else:
        part_copies = [
            pltpu.make_async_copy(slots.at[pl.ds(2 * stride * i, 2 * stride)], part, slot_sem.at[i])
            for i, part in enumerate(parts)
        ]
    for copy in part_copies:
        copy.start()
    query_grad = (acc_ref[...] * (l_ref[...] * score_scale)).astype(jnp.bfloat16)
    for h in range(heads):
        att[:, head_columns(h)] = query_grad[h * NODE_LEN : (h + 1) * NODE_LEN, :]
    dq_out = pltpu.make_async_copy(att, dq_any.at[:, pl.ds(head * width, width)], sem.at[5])
    dq_out.start()
    for copy in part_copies + [own_out]:
        copy.wait()
    proj_out.wait()
    dq_out.wait()


def attention(
    head, chunk_head, head_group, nodes, slot_heads,
    owner_slot, query_rows, own, weight, pieces, near, old, after,
):
    bf16, f32 = jnp.bfloat16, jnp.float32
    stride = nodes // 4
    width = head_group * HEAD_DIM
    rows = head_group * NODE_LEN
    d_out = weight.shape[1]
    block = (NODE_LEN, PAIR)
    anywhere = pl.BlockSpec(memory_space=pl.ANY)
    in_smem = pl.BlockSpec(memory_space=pltpu.SMEM)
    if slot_heads:
        parts = [jax.ShapeDtypeStruct((nodes, slot_heads) + block, bf16)]
    else:
        parts = [jax.ShapeDtypeStruct((2 * stride,) + block, bf16)] * 2
    first_old = 4 + len(pieces) + len(near)
    aliases = {first_old + i: i if i < 2 else 3 for i in range(len(old))}
    layout = (len(pieces), len(near), len(after), chunk_head, bool(slot_heads), len(old), head)
    blocks = (CHAIN + 1) * head_group
    return pl.pallas_call(
        functools.partial(attend, layout),
        in_specs=[in_smem] + [anywhere] * (3 + len(pieces) + len(near) + len(old) + len(after)),
        out_specs=[anywhere] * (3 + len(parts)),
        out_shape=[
            jax.ShapeDtypeStruct(query_rows.shape, bf16),
            jax.ShapeDtypeStruct((NODE_LEN, d_out), f32),
            jax.ShapeDtypeStruct(block, f32),
        ]
        + parts,
        input_output_aliases=aliases,
        scratch_shapes=[
            pltpu.VMEM((CHAIN,) + block, bf16),
            pltpu.VMEM(block, bf16),
            pltpu.VMEM((NODE_LEN, d_out), bf16),
            pltpu.VMEM((width, d_out), bf16),
            pltpu.VMEM((NODE_LEN, d_out), f32),
            pltpu.VMEM((NODE_LEN, width), bf16),
            pltpu.VMEM((CHAIN + 1, rows, NODE_LEN), f32),
            pltpu.VMEM((CHAIN + 1, rows, NODE_LEN), bf16),
            pltpu.VMEM((rows, HEAD_DIM), bf16),
            pltpu.VMEM((rows, HEAD_DIM), bf16),
            pltpu.VMEM((HEAD_DIM, rows), bf16),
            pltpu.VMEM((HEAD_DIM, rows), bf16),
            pltpu.VMEM((rows, HEAD_DIM), f32),
            pltpu.VMEM((rows, HEAD_DIM), f32),
            pltpu.VMEM((rows, HEAD_DIM), f32),
            pltpu.VMEM(block, f32),
            pltpu.VMEM((nodes,) + block, bf16),
            pltpu.SemaphoreType.DMA((2 * CHAIN,)),
            pltpu.SemaphoreType.DMA((2,)),
            pltpu.SemaphoreType.DMA((head_group,)),
            pltpu.SemaphoreType.DMA((2,)),
            pltpu.SemaphoreType.DMA((6,)),
        ],
        compiler_params=pltpu.CompilerParams(vmem_limit_bytes=63 * 1024 * 1024),
        cost_estimate=pl.CostEstimate(
            flops=2 * blocks * NODE_LEN,
            bytes_accessed=2**20,
            transcendentals=0,
        ),
    )(owner_slot, query_rows, own, weight, *pieces, *near, *old, *after)


def zero_of(value):
    return jnp.minimum(jnp.abs(value.reshape(-1)[0].astype(jnp.float32)), 0.0)


def swap(block, mask, nodes):
    return lax.ppermute(block, "node", [(i, i ^ mask) for i in range(nodes)])


def gather_near(own, nodes):
    stride = nodes // 4
    line = jnp.stack([own] + [swap(own, 4 * d, nodes) for d in range(1, stride)])
    cross = swap(line, 2, nodes)
    return [line, swap(line, 1, nodes), cross, swap(cross, 1, nodes)]


def add_level_1(keep, cross, came_keep, came_cross, after, cross_sum, keep_sum):
    f32 = jnp.float32
    cross_sum[...] = (cross[...].astype(f32) + came_cross[...].astype(f32)).astype(jnp.bfloat16)
    keep_sum[...] = keep[...].astype(f32) + came_keep[...].astype(f32)


def add_level_2(keep, came, *refs):
    keep_sum, *sent = refs[1:]
    total = keep[0] + came[0].astype(jnp.float32)
    for d in range(len(sent) + 1):

        @pl.when(pl.program_id(0) == d)
        def _():
            if d == 0:
                keep_sum[...] = total
            else:
                sent[d - 1][...] = total.astype(jnp.bfloat16)


def add_all(*refs):
    *parts, after, total = refs
    total[...] = functools.reduce(jnp.add, [part[...].astype(jnp.float32) for part in parts]).astype(total.dtype)


def small_call(kernel, grid, in_specs, out_specs, out_shape, operands, after):
    return pl.pallas_call(
        kernel,
        grid=grid,
        in_specs=in_specs + [pl.BlockSpec(memory_space=pl.ANY)],
        out_specs=out_specs,
        out_shape=out_shape,
        compiler_params=pltpu.CompilerParams(vmem_limit_bytes=16 * 1024 * 1024),
        cost_estimate=pl.CostEstimate(flops=2**10, bytes_accessed=2**12, transcendentals=0),
    )(*operands, after)


def scatter_sum(kept, away, own_part, nodes):
    bf16, f32 = jnp.bfloat16, jnp.float32
    stride = nodes // 4
    came = swap(away, 1, nodes)
    after = yield [away]
    block = kept.shape[1:]
    one = pl.BlockSpec((1,) + block, lambda d: (d, 0, 0))
    far = pl.BlockSpec((1,) + block, lambda d: (stride + d, 0, 0))
    whole = pl.BlockSpec(block, lambda d: (0, 0))
    cross, keep = small_call(
        add_level_1,
        (stride,),
        [one, far, one, far],
        [one, one],
        [jax.ShapeDtypeStruct((stride,) + block, t) for t in (bf16, f32)],
        [kept, kept, came, came],
        after,
    )
    came = swap(cross, 2, nodes)
    after = yield [cross]
    keep, *sent = small_call(
        add_level_2,
        (stride,),
        [one, one],
        [whole] * stride,
        [jax.ShapeDtypeStruct(block, f32)] + [jax.ShapeDtypeStruct(block, bf16)] * (stride - 1),
        [keep, came],
        after,
    )
    came = [swap(part, 4 * (d + 1), nodes) for d, part in enumerate(sent)]
    after = yield sent
    parts = [own_part, keep] + came
    return small_call(
        add_all, (1,), [whole] * len(parts), whole, jax.ShapeDtypeStruct(block, bf16), parts, after
    )


def local(tp, nodes, query_rows, key_rows, value_rows, out_weight, out_grad, owner_slot):
    bf16, f32 = jnp.bfloat16, jnp.float32
    kv_width = key_rows.shape[1]
    kv_heads = kv_width // HEAD_DIM
    head_group = query_rows.shape[1] // kv_width
    if tp == 2:
        pieces = [out_grad, lax.ppermute(out_grad, "tp", [(0, 1), (1, 0)])]
    else:
        pieces = [lax.all_gather(out_grad, "tp", axis=0, tiled=True)]

    own, near = {}, {}
    for first, heads in [(0, 1)] + ([(1, kv_heads - 1)] if kv_heads > 1 else []):
        columns = slice(first * HEAD_DIM, (first + heads) * HEAD_DIM)
        packed = jnp.concatenate([key_rows[:, columns], value_rows[:, columns]], axis=1)
        if first == 0:
            blocks = gather_near(packed, nodes)
        else:
            blocks = [lax.all_gather(packed, "node", axis=0, tiled=False)]
        for i in range(heads):
            own[first + i], near[first + i] = (packed, i), blocks

    offloaded = max(0, kv_heads - 2)
    old, sums, own_parts, sent = [], [], [], []
    for k in range(kv_heads):
        by_slot = k < offloaded
        dq, proj, own_part, *parts = attention(
            k, own[k][1], head_group, nodes, offloaded if by_slot else 0,
            owner_slot, query_rows, own[k][0], out_weight, pieces, near[k], old, sent,
        )
        old = [dq, proj] + (parts if k + 1 < offloaded else [])
        sent = [own_part]
        if by_slot:
            own_parts.append(own_part)
            if k + 1 == offloaded:
                came = lax.psum_scatter(parts[0], "node", scatter_dimension=0, tiled=False)
        else:
            sums.append(scatter_sum(*parts, own_part, nodes))
            sent = next(sums[-1])
            if k + 1 < kv_heads:
                sent = sums[-1].send(own_part)

    *earlier, last = sums
    early = [chain.send(own_part)[0] for chain in earlier] + [own_part]
    middle = last.send(early[0])[0]
    rows = proj.shape[0] // tp
    if tp == 2:
        me = lax.axis_index("tp")
        away = lax.dynamic_slice_in_dim(proj, (1 - me) * rows, rows, 0)
        away = (away + zero_of(early[0])).astype(bf16)
        here = lax.dynamic_slice_in_dim(proj, me * rows, rows, 0)
        projected = here + lax.ppermute(away, "tp", [(0, 1), (1, 0)]).astype(f32)
        projected = projected.astype(bf16)
    else:
        projected = lax.psum_scatter(proj.astype(bf16), "tp", scatter_dimension=0, tiled=True)
    moved = last.send(middle)[0]
    totals = []
    for chain in earlier + [last]:
        try:
            chain.send(moved)
        except StopIteration as end:
            totals.append(end.value)
    if offloaded:
        totals = [(own_parts[k] + came[k].astype(f32)).astype(bf16) for k in range(offloaded)] + totals
    return (
        projected,
        dq,
        jnp.concatenate([total[:, :HEAD_DIM] for total in totals], axis=1),
        jnp.concatenate([total[:, HEAD_DIM:] for total in totals], axis=1),
    )


def solution(mesh):
    in_specs = (
        P("node", "tp"),
        P("node", "tp"),
        P("node", "tp"),
        P("tp", None),
        P(("node", "tp"), None),
        P(),
    )
    out_specs = (P(("node", "tp"), None), P("node", "tp"), P("node", "tp"), P("node", "tp"))
    return jax.shard_map(
        functools.partial(local, mesh.shape["tp"], mesh.shape["node"]),
        mesh=mesh, in_specs=in_specs, out_specs=out_specs, check_vma=False,
    )
```

profile of v0, /device:TPU:0, one launch (start us, length us, event | category | flops | bytes accessed | tf_op | source)
XLA Modules:
  0.0 227.8 jit_solution(10727614081561551618)
XLA Ops:
  7.2 0.0 slice-start
  7.2 0.0 slice-start.1
  7.2 0.0 copy-start.8
  7.2 0.0 all-gather.3.cloned.1.call-start
  7.2 1.0 slice.47
  8.3 1.0 slice.48
  9.2 0.8 pad_maximum_fusion.1.refs_1_
  10.0 0.0 all-gather.3.cloned.1.call-update
  10.1 0.0 reduce-scatter.2.cloned.1.call-start
  10.1 0.0 copy-start.15
  10.2 3.1 %collective-permute-start.1 = (bf16[256,256]{1,0:T(8,128)(2,1)S(1)}, bf16[256,256]{1,0:T(8,128)(2,1)S(1)}, u32[]{:S(2)}, u32[]{:S(2)}) collective-permute-start(bf16[256,256]{1,0:T(8,128)(2,1)S(1)} %get-tuple-element.75.refs_1_), channel_id=1, source_target_pairs={{0,8},{2,10},{4,12},{6,14},{8,0},{10,2},{12,4},{14,6},{16,24},{18,... | collective-permute-start | bytes 393224 | tf_op jit(solution)/shard_map/ppermute | solution.py:324
  13.3 2.6 %collective-permute-start.2 = (bf16[256,256]{1,0:T(8,128)(2,1)S(1)}, bf16[256,256]{1,0:T(8,128)(2,1)S(1)}, u32[]{:S(2)}, u32[]{:S(2)}) collective-permute-start(bf16[256,256]{1,0:T(8,128)(2,1)S(1)} %get-tuple-element.75.refs_1_), channel_id=1, source_target_pairs={{0,16},{2,18},{4,20},{6,22},{8,24},{10,26},{12,28},{14,30},{16,0},... | collective-permute-start | bytes 393224 | tf_op jit(solution)/shard_map/ppermute | solution.py:324
  15.8 2.4 %collective-permute-done.1 = bf16[256,256]{1,0:T(8,128)(2,1)S(1)} collective-permute-done((bf16[256,256]{1,0:T(8,128)(2,1)S(1)}, bf16[256,256]{1,0:T(8,128)(2,1)S(1)}, u32[]{:S(2)}, u32[]{:S(2)}) %collective-permute-start.1) | collective-permute-done | bytes 131104 | tf_op jit(solution)/shard_map/ppermute | solution.py:324
  18.3 10.5 %collective-permute-done.2 = bf16[256,256]{1,0:T(8,128)(2,1)S(1)} collective-permute-done((bf16[256,256]{1,0:T(8,128)(2,1)S(1)}, bf16[256,256]{1,0:T(8,128)(2,1)S(1)}, u32[]{:S(2)}, u32[]{:S(2)}) %collective-permute-start.2) | collective-permute-done | bytes 131104 | tf_op jit(solution)/shard_map/ppermute | solution.py:324
  28.8 0.0 collective-permute-done.3
  28.8 0.1 pad_maximum_fusion.refs_5_
  28.9 1.6 collective-permute-start.5
  30.5 1.7 collective-permute-start
  32.2 7.0 %collective-permute-done.5.refs_7_ = bf16[4,256,256]{2,1,0:T(8,128)(2,1)S(1)} collective-permute-done((bf16[4,256,256]{2,1,0:T(8,128)(2,1)S(1)}, bf16[4,256,256]{2,1,0:T(8,128)(2,1)S(1)}, u32[]{:S(2)}, u32[]{:S(2)}) %collective-permute-start.5) | collective-permute-done | bytes 524320 | tf_op jit(solution)/shard_map/ppermute | solution.py:324
  39.2 0.0 collective-permute-start.6
  39.2 0.0 collective-permute-done.4.refs_6_
  39.2 10.7 %collective-permute-done.refs_4_ = bf16[128,4096]{1,0:T(8,128)(2,1)S(1)} collective-permute-done((bf16[128,4096]{1,0:T(8,128)(2,1)S(1)}, bf16[128,4096]{1,0:T(8,128)(2,1)S(1)}, u32[]{:S(2)}, u32[]{:S(2)}) %collective-permute-start) | collective-permute-done | bytes 1048608 | tf_op jit(solution)/shard_map/ppermute | solution.py:413
  50.0 1.0 copy-done.9
  51.0 0.0 collective-permute-done.6.refs_8_
  51.0 14.2 %shard_map.93 = (bf16[256,4096]{1,0:T(8,128)(2,1)}, f32[256,4096]{1,0:T(8,128)}, f32[256,256]{1,0:T(8,128)}, bf16[16,2,256,256]{3,2,1,0:T(8,128)(2,1)}) custom-call(s32[16]{0:T(128)} %owner_slot.7, bf16[256,4096]{1,0:T(8,128)(2,1)} %refs_0_.7, bf16[256,256]{1,0:T(8,128)(2,1)} %copy-done.15, bf16[4096,4096]{1,0:T(8,128)(2,1)} %refs_2_.7, ...), custom_call_target="tpu_custom_call" | custom-call | flops 36864 | bytes 1048576 | tf_op jit(solution)/shard_map/pallas_call | solution.py:275
  65.2 13.2 %all-gather.3.cloned.1.call-done = bf16[4096,768]{1,0:T(8,128)(2,1)} async-done(((bf16[256,768]{1,0:T(8,128)(2,1)}), bf16[4096,768]{1,0:T(8,128)(2,1)}) %all-gather.3.cloned.1.call-update) | async-done | bytes 6291472 | tf_op jit(solution)/shard_map/all_gather | solution.py:424
  78.4 15.4 %shard_map.94 = (bf16[256,4096]{1,0:T(8,128)(2,1)}, f32[256,4096]{1,0:T(8,128)}, f32[256,256]{1,0:T(8,128)}, bf16[16,2,256,256]{3,2,1,0:T(8,128)(2,1)}) custom-call(s32[16]{0:T(128)} %owner_slot.7, bf16[256,4096]{1,0:T(8,128)(2,1)} %refs_0_.7, ...), custom_call_target="tpu_custom_call", output_to_operand_aliasing={{0}: (7, {}), {1}: (8, {}), {3}: (9, {})} | custom-call | flops 36864 | bytes 1048576 | tf_op jit(solution)/shard_map/pallas_call | solution.py:275
  93.8 0.0 reduce-scatter.2.cloned.1.call-update
  93.8 15.5 %shard_map.95 = (bf16[256,4096]{1,0:T(8,128)(2,1)}, f32[256,4096]{1,0:T(8,128)}, f32[256,256]{1,0:T(8,128)}, bf16[8,256,256]{2,1,0:T(8,128)(2,1)}, bf16[8,256,256]{2,1,0:T(8,128)(2,1)}) custom-call(s32[16]{0:T(128)} %owner_slot.7, bf16[256,4096]{1,0:T(8,128)(2,1)} %refs_0_.7, ...), custom_call_target="tpu_custom_call", output_to_operand_aliasing={{0}: (7, {}), {1}: (8, {})} | custom-call | flops 36864 | bytes 1048576 | tf_op jit(solution)/shard_map/pallas_call | solution.py:275
  109.2 26.7 %collective-permute-start.7 = (bf16[8,256,256]{2,1,0:T(8,128)(2,1)}, bf16[8,256,256]{2,1,0:T(8,128)(2,1)S(1)}, u32[]{:S(2)}, u32[]{:S(2)}) collective-permute-start(bf16[8,256,256]{2,1,0:T(8,128)(2,1)} %get-tuple-element.44), channel_id=1, source_target_pairs={{0,2},{2,0},{4,6},{6,4},{8,10},{10,8},{12,14},{14,12},{16,18},{18,... | collective-permute-start | bytes 3145736 | tf_op jit(solution)/shard_map/ppermute | solution.py:324
  136.0 2.5 %collective-permute-done.7.came_keep.came_cross = bf16[8,256,256]{2,1,0:T(8,128)(2,1)S(1)} collective-permute-done((bf16[8,256,256]{2,1,0:T(8,128)(2,1)}, bf16[8,256,256]{2,1,0:T(8,128)(2,1)S(1)}, u32[]{:S(2)}, u32[]{:S(2)}) %collective-permute-start.7) | collective-permute-done | bytes 1048608 | tf_op jit(solution)/shard_map/ppermute | solution.py:324
  138.5 1.2 copy-done
  139.7 0.9 copy-done.6
  140.7 1.4 shard_map.96
  142.1 1.0 copy-done.2
  143.1 0.0 collective-permute-start.8
  143.1 15.9 %shard_map.97 = (bf16[256,4096]{1,0:T(8,128)(2,1)}, f32[256,4096]{1,0:T(8,128)}, f32[256,256]{1,0:T(8,128)}, bf16[8,256,256]{2,1,0:T(8,128)(2,1)}, bf16[8,256,256]{2,1,0:T(8,128)(2,1)}) custom-call(s32[16]{0:T(128)} %owner_slot.7, bf16[256,4096]{1,0:T(8,128)(2,1)} %refs_0_.7, ...), custom_call_target="tpu_custom_call", output_to_operand_aliasing={{0}: (7, {}), {1}: (8, {})} | custom-call | flops 36864 | bytes 1048576 | tf_op jit(solution)/shard_map/pallas_call | solution.py:275
  159.0 12.9 %collective-permute-start.13 = (bf16[8,256,256]{2,1,0:T(8,128)(2,1)}, bf16[8,256,256]{2,1,0:T(8,128)(2,1)S(1)}, u32[]{:S(2)}, u32[]{:S(2)}) collective-permute-start(bf16[8,256,256]{2,1,0:T(8,128)(2,1)} %get-tuple-element.57), channel_id=1, source_target_pairs={{0,2},{2,0},{4,6},{6,4},{8,10},{10,8},{12,14},{14,12},{16,18},{18,... | collective-permute-start | bytes 3145736 | tf_op jit(solution)/shard_map/ppermute | solution.py:324
  171.9 1.2 copy-done.3
  173.2 0.9 copy-done.4
  174.1 0.9 shard_map.98
  175.0 0.1 copy.17
  175.1 0.5 slice.62
  176.3 2.7 %add_convert_fusion.1 = bf16[128,4096]{1,0:T(8,128)(2,1)} fusion(f32[256,4096]{1,0:T(8,128)} %get-tuple-element.47, s32[]{:T(128)S(6)} %select_n.7, f32[]{:T(128)} %bitcast.5), kind=kLoop, calls=%fused_computation.1 | loop fusion | flops 1048576 | bytes 3145736 | tf_op jit(solution)/shard_map/convert_element_type | solution.py:455
  179.1 1.5 collective-permute-start.9
  180.6 0.3 shard_map.99
  180.9 0.1 collective-permute-start.14
  181.0 9.6 %collective-permute-start.10 = (bf16[256,256]{1,0:T(8,128)(2,1)S(1)}, bf16[256,256]{1,0:T(8,128)(2,1)S(1)}, u32[]{:S(2)}, u32[]{:S(2)}) collective-permute-start(bf16[256,256]{1,0:T(8,128)(2,1)S(1)} %get-tuple-element.50.after), channel_id=1, source_target_pairs={{0,8},{2,10},{4,12},{6,14},{8,0},{10,2},{12,4},{14,6},{16,24},{18,... | collective-permute-start | bytes 393224 | tf_op jit(solution)/shard_map/ppermute | solution.py:324
  190.5 4.0 %collective-permute-start.11 = (bf16[256,256]{1,0:T(8,128)(2,1)}, bf16[256,256]{1,0:T(8,128)(2,1)S(1)}, u32[]{:S(2)}, u32[]{:S(2)}) collective-permute-start(bf16[256,256]{1,0:T(8,128)(2,1)} %get-tuple-element.54), channel_id=1, source_target_pairs={{0,16},{2,18},{4,20},{6,22},{8,24},{10,26},{12,28},{14,30},{16,0},... | collective-permute-start | bytes 393224 | tf_op jit(solution)/shard_map/ppermute | solution.py:324
  194.5 1.5 collective-permute-start.12
  196.0 1.3 collective-permute-done.14.came
  197.3 0.2 shard_map.100
  197.5 7.0 %collective-permute-start.15 = (bf16[256,256]{1,0:T(8,128)(2,1)S(1)}, bf16[256,256]{1,0:T(8,128)(2,1)S(1)}, u32[]{:S(2)}, u32[]{:S(2)}) collective-permute-start(bf16[256,256]{1,0:T(8,128)(2,1)S(1)} %get-tuple-element.60.refs_5_), channel_id=1, source_target_pairs={{0,8},{2,10},{4,12},{6,14},{8,0},{10,2},{12,4},{14,6},{16,24},{18,... | collective-permute-start | bytes 393224 | tf_op jit(solution)/shard_map/ppermute | solution.py:324
  204.6 2.5 %collective-permute-start.16 = (bf16[256,256]{1,0:T(8,128)(2,1)S(1)}, bf16[256,256]{1,0:T(8,128)(2,1)S(1)}, u32[]{:S(2)}, u32[]{:S(2)}) collective-permute-start(bf16[256,256]{1,0:T(8,128)(2,1)S(1)} %get-tuple-element.62), channel_id=1, source_target_pairs={{0,16},{2,18},{4,20},{6,22},{8,24},{10,26},{12,28},{14,30},{16,0},... | collective-permute-start | bytes 393224 | tf_op jit(solution)/shard_map/ppermute | solution.py:324
  207.1 3.1 %collective-permute-start.17 = (bf16[256,256]{1,0:T(8,128)(2,1)S(1)}, bf16[256,256]{1,0:T(8,128)(2,1)S(1)}, u32[]{:S(2)}, u32[]{:S(2)}) collective-permute-start(bf16[256,256]{1,0:T(8,128)(2,1)S(1)} %get-tuple-element.63), channel_id=1, source_target_pairs={{0,24},{2,26},{4,28},{6,30},{8,16},{10,18},{12,20},{14,22},{16,8},... | collective-permute-start | bytes 393224 | tf_op jit(solution)/shard_map/ppermute | solution.py:324
  210.2 1.0 shard_map.101
  211.2 0.0 copy-start.11
  211.2 0.0 copy-start.12
  211.2 3.2 %add_convert_fusion = bf16[128,4096]{1,0:T(8,128)(2,1)} fusion(bf16[128,4096]{1,0:T(8,128)(2,1)} %collective-permute-done.9, f32[256,4096]{1,0:T(8,128)} %get-tuple-element.47, s32[]{:T(128)S(6)} %select_n.6), kind=kLoop, calls=%fused_computation | loop fusion | flops 1572864 | bytes 4194308 | tf_op jit(solution)/shard_map/convert_element_type | solution.py:458
  214.4 4.4 %collective-permute-done.16.refs_3_ = bf16[256,256]{1,0:T(8,128)(2,1)S(1)} collective-permute-done((bf16[256,256]{1,0:T(8,128)(2,1)S(1)}, bf16[256,256]{1,0:T(8,128)(2,1)S(1)}, u32[]{:S(2)}, u32[]{:S(2)}) %collective-permute-start.16) | collective-permute-done | bytes 131104 | tf_op jit(solution)/shard_map/ppermute | solution.py:324
  218.9 0.1 shard_map.102
  219.0 0.0 reduce-scatter.2.cloned.1.call-done
  219.0 1.0 fusion.1
  220.1 0.9 pad_maximum_fusion.2
  (39 shorter events, 0.1 us)
Async XLA Ops:
  7.2 2.9 %slice-start = ((bf16[256,512]{1,0:T(8,128)(2,1)}), bf16[256,128]{1,0:T(8,128)(2,1)S(1)}, s32[]{:S(2)}) async-start(bf16[256,512]{1,0:T(8,128)(2,1)} %param.7), calls=%async_computation.3 | async-start | bytes 131072 | tf_op jit(solution)/shard_map/slice | solution.py:420
  7.2 2.9 %slice-start.1 = ((bf16[256,512]{1,0:T(8,128)(2,1)}), bf16[256,128]{1,0:T(8,128)(2,1)S(1)}, s32[]{:S(2)}) async-start(bf16[256,512]{1,0:T(8,128)(2,1)} %param.8), calls=%async_computation.4 | async-start | bytes 131072 | tf_op jit(solution)/shard_map/slice | solution.py:420
  7.2 23.3 %copy-start.8 = (bf16[128,4096]{1,0:T(8,128)(2,1)S(1)}, bf16[128,4096]{1,0:T(8,128)(2,1)}, u32[]{:S(2)}) copy-start(bf16[128,4096]{1,0:T(8,128)(2,1)} %refs_3_.7) | copy-start | bytes 3145732
  7.2 71.2 %all-gather.3.cloned.1.call-start = ((), (), s32[]{:S(2)}) async-start(), calls=%async_computation.2 | async-start | bytes 6684672 | tf_op jit(solution)/shard_map/all_gather | solution.py:424
  10.1 208.9 %reduce-scatter.2.cloned.1.call-start = ((), (), s32[]{:S(2)}) async-start(), calls=%async_computation.1 | async-start | bytes 4456448 | tf_op jit(solution)/shard_map/reduce_scatter | solution.py:441
  10.1 40.8 %copy-start.15 = (bf16[256,256]{1,0:T(8,128)(2,1)}, bf16[256,256]{1,0:T(8,128)(2,1)S(1)}, u32[]{:S(2)}) copy-start(bf16[256,256]{1,0:T(8,128)(2,1)S(1)} %get-tuple-element.75.refs_1_) | copy-start | bytes 393220
  10.2 8.1 %collective-permute-start.1 = (bf16[256,256]{1,0:T(8,128)(2,1)S(1)}, bf16[256,256]{1,0:T(8,128)(2,1)S(1)}, u32[]{:S(2)}, u32[]{:S(2)}) collective-permute-start(bf16[256,256]{1,0:T(8,128)(2,1)S(1)} %get-tuple-element.75.refs_1_), channel_id=1, source_target_pairs={{0,8},{2,10},{4,12},{6,14},{8,0},{10,2},{12,4},{14,6},{16,24},{18,... | collective-permute-start | bytes 393224 | tf_op jit(solution)/shard_map/ppermute | solution.py:324
  13.3 15.6 %collective-permute-start.2 = (bf16[256,256]{1,0:T(8,128)(2,1)S(1)}, bf16[256,256]{1,0:T(8,128)(2,1)S(1)}, u32[]{:S(2)}, u32[]{:S(2)}) collective-permute-start(bf16[256,256]{1,0:T(8,128)(2,1)S(1)} %get-tuple-element.75.refs_1_), channel_id=1, source_target_pairs={{0,16},{2,18},{4,20},{6,22},{8,24},{10,26},{12,28},{14,30},{16,0},... | collective-permute-start | bytes 393224 | tf_op jit(solution)/shard_map/ppermute | solution.py:324
  15.8 13.0 %collective-permute-start.3 = (bf16[256,256]{1,0:T(8,128)(2,1)S(1)}, bf16[256,256]{1,0:T(8,128)(2,1)S(1)}, u32[]{:S(2)}, u32[]{:S(2)}) collective-permute-start(bf16[256,256]{1,0:T(8,128)(2,1)S(1)} %get-tuple-element.75.refs_1_), channel_id=1, source_target_pairs={{0,24},{2,26},{4,28},{6,30},{8,16},{10,18},{12,20},{14,22},{16,8},... | collective-permute-start | bytes 393224 | tf_op jit(solution)/shard_map/ppermute | solution.py:324
  28.9 22.1 %copy-start.10 = (bf16[4,256,256]{2,1,0:T(8,128)(2,1)}, bf16[4,256,256]{2,1,0:T(8,128)(2,1)S(1)}, u32[]{:S(2)}) copy-start(bf16[4,256,256]{2,1,0:T(8,128)(2,1)S(1)} %pad_maximum_fusion.refs_5_) | copy-start | bytes 1572868
  28.9 10.3 %collective-permute-start.5 = (bf16[4,256,256]{2,1,0:T(8,128)(2,1)S(1)}, bf16[4,256,256]{2,1,0:T(8,128)(2,1)S(1)}, u32[]{:S(2)}, u32[]{:S(2)}) collective-permute-start(bf16[4,256,256]{2,1,0:T(8,128)(2,1)S(1)} %pad_maximum_fusion.refs_5_), channel_id=1, source_target_pairs={{0,4},{2,6},{4,0},{6,2},{8,12},{10,14},{12,8},{14,10},{16,20},{18,... | collective-permute-start | bytes 1572872 | tf_op jit(solution)/shard_map/ppermute | solution.py:324
  30.5 19.5 %collective-permute-start = (bf16[128,4096]{1,0:T(8,128)(2,1)S(1)}, bf16[128,4096]{1,0:T(8,128)(2,1)S(1)}, u32[]{:S(2)}, u32[]{:S(2)}) collective-permute-start(bf16[128,4096]{1,0:T(8,128)(2,1)S(1)} %copy-done.8), channel_id=1, source_target_pairs={{0,1},{1,0},{2,3},{3,2},{4,5},{5,4},{6,7},{7,6},{8,9},{9,8},{10,11... | collective-permute-start | bytes 3145736 | tf_op jit(solution)/shard_map/ppermute | solution.py:413
  32.2 7.1 %collective-permute-start.4 = (bf16[4,256,256]{2,1,0:T(8,128)(2,1)S(1)}, bf16[4,256,256]{2,1,0:T(8,128)(2,1)S(1)}, u32[]{:S(2)}, u32[]{:S(2)}) collective-permute-start(bf16[4,256,256]{2,1,0:T(8,128)(2,1)S(1)} %pad_maximum_fusion.refs_5_), channel_id=1, source_target_pairs={{0,2},{2,0},{4,6},{6,4},{8,10},{10,8},{12,14},{14,12},{16,18},{18,... | collective-permute-start | bytes 1572872 | tf_op jit(solution)/shard_map/ppermute | solution.py:324
  39.2 10.8 %copy-start.13 = (bf16[4,256,256]{2,1,0:T(8,128)(2,1)}, bf16[4,256,256]{2,1,0:T(8,128)(2,1)S(1)}, u32[]{:S(2)}) copy-start(bf16[4,256,256]{2,1,0:T(8,128)(2,1)S(1)} %collective-permute-done.5.refs_7_) | copy-start | bytes 1572868
  39.2 11.7 %collective-permute-start.6 = (bf16[4,256,256]{2,1,0:T(8,128)(2,1)S(1)}, bf16[4,256,256]{2,1,0:T(8,128)(2,1)}, u32[]{:S(2)}, u32[]{:S(2)}) collective-permute-start(bf16[4,256,256]{2,1,0:T(8,128)(2,1)S(1)} %collective-permute-done.5.refs_7_), channel_id=1, source_target_pairs={{0,2},{2,0},{4,6},{6,4},{8,10},{10,8},{12,14},{14,12},{16,18},{18,... | collective-permute-start | bytes 1572872 | tf_op jit(solution)/shard_map/ppermute | solution.py:324
  39.2 10.8 %copy-start.14 = (bf16[4,256,256]{2,1,0:T(8,128)(2,1)}, bf16[4,256,256]{2,1,0:T(8,128)(2,1)S(1)}, u32[]{:S(2)}) copy-start(bf16[4,256,256]{2,1,0:T(8,128)(2,1)S(1)} %collective-permute-done.4.refs_6_) | copy-start | bytes 1572868
  50.0 1.0 copy-start.9
  109.2 29.2 %collective-permute-start.7 = (bf16[8,256,256]{2,1,0:T(8,128)(2,1)}, bf16[8,256,256]{2,1,0:T(8,128)(2,1)S(1)}, u32[]{:S(2)}, u32[]{:S(2)}) collective-permute-start(bf16[8,256,256]{2,1,0:T(8,128)(2,1)} %get-tuple-element.44), channel_id=1, source_target_pairs={{0,2},{2,0},{4,6},{6,4},{8,10},{10,8},{12,14},{14,12},{16,18},{18,... | collective-permute-start | bytes 3145736 | tf_op jit(solution)/shard_map/ppermute | solution.py:324
  138.5 1.2 copy-start
  139.7 0.9 copy-start.6
  142.1 1.0 copy-start.2
  143.1 28.8 %collective-permute-start.8 = (bf16[4,256,256]{2,1,0:T(8,128)(2,1)}, bf16[4,256,256]{2,1,0:T(8,128)(2,1)S(1)}, u32[]{:S(2)}, u32[]{:S(2)}) collective-permute-start(bf16[4,256,256]{2,1,0:T(8,128)(2,1)} %get-tuple-element.46.refs_8_), channel_id=1, source_target_pairs={{0,4},{2,6},{4,0},{6,2},{8,12},{10,14},{12,8},{14,10},{16,20},{18,... | collective-permute-start | bytes 1572872 | tf_op jit(solution)/shard_map/ppermute | solution.py:324
  159.0 21.6 %collective-permute-start.13 = (bf16[8,256,256]{2,1,0:T(8,128)(2,1)}, bf16[8,256,256]{2,1,0:T(8,128)(2,1)S(1)}, u32[]{:S(2)}, u32[]{:S(2)}) collective-permute-start(bf16[8,256,256]{2,1,0:T(8,128)(2,1)} %get-tuple-element.57), channel_id=1, source_target_pairs={{0,2},{2,0},{4,6},{6,4},{8,10},{10,8},{12,14},{14,12},{16,18},{18,... | collective-permute-start | bytes 3145736 | tf_op jit(solution)/shard_map/ppermute | solution.py:324
  171.9 1.2 copy-start.3
  173.2 0.9 copy-start.4
  175.0 5.6 %copy-start.1 = (bf16[8,256,256]{2,1,0:T(8,128)(2,1)S(1)}, bf16[8,256,256]{2,1,0:T(8,128)(2,1)}, u32[]{:S(2)}) copy-start(bf16[8,256,256]{2,1,0:T(8,128)(2,1)} %get-tuple-element.56.keep.cross) | copy-start | bytes 3145732
  179.1 32.2 %collective-permute-start.9 = (bf16[128,4096]{1,0:T(8,128)(2,1)}, bf16[128,4096]{1,0:T(8,128)(2,1)}, u32[]{:S(2)}, u32[]{:S(2)}) collective-permute-start(bf16[128,4096]{1,0:T(8,128)(2,1)} %add_convert_fusion.1), channel_id=1, source_target_pairs={{0,1},{1,0},{2,3},{3,2},{4,5},{5,4},{6,7},{7,6},{8,9},{9,8},{10,11... | collective-permute-start | bytes 3145736 | tf_op jit(solution)/shard_map/ppermute | solution.py:457
  180.9 29.3 %copy-start.7 = (f32[256,256]{1,0:T(8,128)S(1)}, f32[256,256]{1,0:T(8,128)}, u32[]{:S(2)}) copy-start(f32[256,256]{1,0:T(8,128)} %get-tuple-element.45.after.refs_0_) | copy-start | bytes 786436
  180.9 16.4 %collective-permute-start.14 = (bf16[4,256,256]{2,1,0:T(8,128)(2,1)S(1)}, bf16[4,256,256]{2,1,0:T(8,128)(2,1)S(1)}, u32[]{:S(2)}, u32[]{:S(2)}) collective-permute-start(bf16[4,256,256]{2,1,0:T(8,128)(2,1)S(1)} %get-tuple-element.59.refs_0_), channel_id=1, source_target_pairs={{0,4},{2,6},{4,0},{6,2},{8,12},{10,14},{12,8},{14,10},{16,20},{18,... | collective-permute-start | bytes 1572872 | tf_op jit(solution)/shard_map/ppermute | solution.py:324
  181.0 23.6 %collective-permute-start.10 = (bf16[256,256]{1,0:T(8,128)(2,1)S(1)}, bf16[256,256]{1,0:T(8,128)(2,1)S(1)}, u32[]{:S(2)}, u32[]{:S(2)}) collective-permute-start(bf16[256,256]{1,0:T(8,128)(2,1)S(1)} %get-tuple-element.50.after), channel_id=1, source_target_pairs={{0,8},{2,10},{4,12},{6,14},{8,0},{10,2},{12,4},{14,6},{16,24},{18,... | collective-permute-start | bytes 393224 | tf_op jit(solution)/shard_map/ppermute | solution.py:324
  190.5 16.5 %collective-permute-start.11 = (bf16[256,256]{1,0:T(8,128)(2,1)}, bf16[256,256]{1,0:T(8,128)(2,1)S(1)}, u32[]{:S(2)}, u32[]{:S(2)}) collective-permute-start(bf16[256,256]{1,0:T(8,128)(2,1)} %get-tuple-element.54), channel_id=1, source_target_pairs={{0,16},{2,18},{4,20},{6,22},{8,24},{10,26},{12,28},{14,30},{16,0},... | collective-permute-start | bytes 393224 | tf_op jit(solution)/shard_map/ppermute | solution.py:324
  194.5 15.7 %collective-permute-start.12 = (bf16[256,256]{1,0:T(8,128)(2,1)}, bf16[256,256]{1,0:T(8,128)(2,1)}, u32[]{:S(2)}, u32[]{:S(2)}) collective-permute-start(bf16[256,256]{1,0:T(8,128)(2,1)} %get-tuple-element.55), channel_id=1, source_target_pairs={{0,24},{2,26},{4,28},{6,30},{8,16},{10,18},{12,20},{14,22},{16,8},... | collective-permute-start | bytes 393224 | tf_op jit(solution)/shard_map/ppermute | solution.py:324
  197.5 16.9 %collective-permute-start.15 = (bf16[256,256]{1,0:T(8,128)(2,1)S(1)}, bf16[256,256]{1,0:T(8,128)(2,1)S(1)}, u32[]{:S(2)}, u32[]{:S(2)}) collective-permute-start(bf16[256,256]{1,0:T(8,128)(2,1)S(1)} %get-tuple-element.60.refs_5_), channel_id=1, source_target_pairs={{0,8},{2,10},{4,12},{6,14},{8,0},{10,2},{12,4},{14,6},{16,24},{18,... | collective-permute-start | bytes 393224 | tf_op jit(solution)/shard_map/ppermute | solution.py:324
  204.6 14.3 %collective-permute-start.16 = (bf16[256,256]{1,0:T(8,128)(2,1)S(1)}, bf16[256,256]{1,0:T(8,128)(2,1)S(1)}, u32[]{:S(2)}, u32[]{:S(2)}) collective-permute-start(bf16[256,256]{1,0:T(8,128)(2,1)S(1)} %get-tuple-element.62), channel_id=1, source_target_pairs={{0,16},{2,18},{4,20},{6,22},{8,24},{10,26},{12,28},{14,30},{16,0},... | collective-permute-start | bytes 393224 | tf_op jit(solution)/shard_map/ppermute | solution.py:324
  207.1 11.8 %collective-permute-start.17 = (bf16[256,256]{1,0:T(8,128)(2,1)S(1)}, bf16[256,256]{1,0:T(8,128)(2,1)S(1)}, u32[]{:S(2)}, u32[]{:S(2)}) collective-permute-start(bf16[256,256]{1,0:T(8,128)(2,1)S(1)} %get-tuple-element.63), channel_id=1, source_target_pairs={{0,24},{2,26},{4,28},{6,30},{8,16},{10,18},{12,20},{14,22},{16,8},... | collective-permute-start | bytes 393224 | tf_op jit(solution)/shard_map/ppermute | solution.py:324
  211.2 7.7 %copy-start.5 = (f32[256,256]{1,0:T(8,128)S(1)}, f32[256,256]{1,0:T(8,128)}, u32[]{:S(2)}) copy-start(f32[256,256]{1,0:T(8,128)} %get-tuple-element.49.refs_0_) | copy-start | bytes 786436
  211.2 7.8 %copy-start.11 = (f32[256,256]{1,0:T(8,128)S(1)}, f32[256,256]{1,0:T(8,128)}, u32[]{:S(2)}) copy-start(f32[256,256]{1,0:T(8,128)} %get-tuple-element.37.refs_9_) | copy-start | bytes 786436
  211.2 7.8 %copy-start.12 = (f32[256,256]{1,0:T(8,128)S(1)}, f32[256,256]{1,0:T(8,128)}, u32[]{:S(2)}) copy-start(f32[256,256]{1,0:T(8,128)} %get-tuple-element.40.refs_8_) | copy-start | bytes 786436
Sparse Core Ops, SparseCore 0:
  10.3 68.0 all-gather.2
  93.9 109.4 reduce-scatter.1
where the time goes:
time: 228 us
  starting transfers between devices  78 us (34%)
  Pallas kernels  64.8 us (28%)
  waiting for transfers between devices  52.3 us (23%)
  between operations  15 us (7%)
  local copies, waits for them, and re-layouts  9.04 us (4%)
  other arithmetic  8.65 us (4%)
    ppermute x16, starting transfers between devices, swap(): return lax.ppermute(block, 'node', [(i, i ^ mask) for i in range(nodes)])  74.7 us
    pallas_call x4, Pallas kernels, attention(): pl.pallas_call(functools.partial(attend, layout), in_specs=[in_smem] + [a...  60.9 us
    ppermute x16, waiting for transfers between devices, swap(): return lax.ppermute(block, 'node', [(i, i ^ mask) for i in range(nodes)])  28.3 us
    all_gather x1, waiting for transfers between devices, local(): blocks = [lax.all_gather(packed, 'node', axis=0, tiled=False)]  13.2 us
    ppermute x1, waiting for transfers between devices, local(): pieces = [out_grad, lax.ppermute(out_grad, 'tp', [(0, 1), (1, 0)])]  10.7 us
    unnamed x33, local copies, waits for them, and re-layouts  6.49 us
  transfers between devices with their start and end apart: 20, of which 8 were waited for; matrix products, arithmetic and copies ran while one was open for 3% of the time, Pallas kernels for 22%

commit v1 on v0

--- a/solution.py
+++ b/solution.py
@@ -324,21 +324,20 @@
     return lax.ppermute(block, "node", [(i, i ^ mask) for i in range(nodes)])
 
 
-def gather_near(own, nodes):
+def gather_near(own, nodes, before):
     stride = nodes // 4
     line = jnp.stack([own] + [swap(own, 4 * d, nodes) for d in range(1, stride)])
-    cross = swap(line, 2, nodes)
+    cross = swap(line, 2, nodes) + zero_of(before).astype(line.dtype)
     return [line, swap(line, 1, nodes), cross, swap(cross, 1, nodes)]
 
 
-def add_level_1(keep, cross, came_keep, came_cross, after, cross_sum, keep_sum):
+def add_level_1(keep, cross, came_keep, came_cross, cross_sum, keep_sum):
     f32 = jnp.float32
     cross_sum[...] = (cross[...].astype(f32) + came_cross[...].astype(f32)).astype(jnp.bfloat16)
     keep_sum[...] = keep[...].astype(f32) + came_keep[...].astype(f32)
 
 
-def add_level_2(keep, came, *refs):
-    keep_sum, *sent = refs[1:]
+def add_level_2(keep, came, keep_sum, *sent):
     total = keep[0] + came[0].astype(jnp.float32)
     for d in range(len(sent) + 1):
 
@@ -351,20 +350,23 @@
 
 
 def add_all(*refs):
-    *parts, after, total = refs
+    *parts, total = refs
     total[...] = functools.reduce(jnp.add, [part[...].astype(jnp.float32) for part in parts]).astype(total.dtype)
 
 
 def small_call(kernel, grid, in_specs, out_specs, out_shape, operands, after):
+    def run(*refs):
+        kernel(*refs[: len(operands)], *refs[len(operands) + len(after) :])
+
     return pl.pallas_call(
-        kernel,
+        run,
         grid=grid,
-        in_specs=in_specs + [pl.BlockSpec(memory_space=pl.ANY)],
+        in_specs=in_specs + [pl.BlockSpec(memory_space=pl.ANY)] * len(after),
         out_specs=out_specs,
         out_shape=out_shape,
         compiler_params=pltpu.CompilerParams(vmem_limit_bytes=16 * 1024 * 1024),
         cost_estimate=pl.CostEstimate(flops=2**10, bytes_accessed=2**12, transcendentals=0),
-    )(*operands, after)
+    )(*operands, *after)
 
 
 def scatter_sum(kept, away, own_part, nodes):
@@ -419,7 +421,7 @@
         columns = slice(first * HEAD_DIM, (first + heads) * HEAD_DIM)
         packed = jnp.concatenate([key_rows[:, columns], value_rows[:, columns]], axis=1)
         if first == 0:
-            blocks = gather_near(packed, nodes)
+            blocks = gather_near(packed, nodes, pieces[-1])
         else:
             blocks = [lax.all_gather(packed, "node", axis=0, tiled=False)]
         for i in range(heads):
@@ -443,11 +445,11 @@
             sums.append(scatter_sum(*parts, own_part, nodes))
             sent = next(sums[-1])
             if k + 1 < kv_heads:
-                sent = sums[-1].send(own_part)
+                sent = sums[-1].send([])
 
     *earlier, last = sums
-    early = [chain.send(own_part)[0] for chain in earlier] + [own_part]
-    middle = last.send(early[0])[0]
+    early = [chain.send([own_part])[0] for chain in earlier] + [own_part]
+    middle = last.send([early[0]])[0]
     rows = proj.shape[0] // tp
     if tp == 2:
         me = lax.axis_index("tp")
@@ -458,11 +460,11 @@
         projected = projected.astype(bf16)
     else:
         projected = lax.psum_scatter(proj.astype(bf16), "tp", scatter_dimension=0, tiled=True)
-    moved = last.send(middle)[0]
+    moved = last.send([middle])[0]
     totals = []
     for chain in earlier + [last]:
         try:
-            chain.send(moved)
+            chain.send([moved] if chain is last else [moved, projected])
         except StopIteration as end:
             totals.append(end.value)
     if offloaded:

time: 228 us -> 228 us (level)
  starting transfers between devices: 78 us -> 64 us
  Pallas kernels: 64.8 us -> 72.9 us
  waiting for transfers between devices: 52.3 us -> 56.4 us
    ppermute x16, starting transfers between devices: 74.7 us -> 59.4 us  [swap(): return lax.ppermute(block, 'node', [(i, i ^ mask) for i in range(nodes)])]
    pallas_call x4, Pallas kernels: 60.9 us -> 70 us  [attention(): pl.pallas_call(functools.partial(attend, layout), in_specs=[in_smem] + [a...]
    ppermute x1, waiting for transfers between devices: 10.7 us -> 2.69 us  [local(): pieces = [out_grad, lax.ppermute(out_grad, 'tp', [(0, 1), (1, 0)])]]
    all_gather x1, waiting for transfers between devices: 13.2 us -> 19.4 us  [local(): blocks = [lax.all_gather(packed, 'node', axis=0, tiled=False)]]
    ppermute x16, waiting for transfers between devices: 28.3 us -> 34.3 us  [swap(): return lax.ppermute(block, 'node', [(i, i ^ mask) for i in range(nodes)])]
    unnamed x33 -> x32, local copies, waits for them, and re-layouts: 6.49 us -> 7.27 us
  transfers between devices with their start and end apart: 20 -> 20, of which waited for: 8 -> 11; matrix products, arithmetic and copies ran while one was open for 3% -> 3% of each run, Pallas kernels for 22% -> 24%
where the time goes in v1:
time: 228 us; the launch traced here: 227 us
  Pallas kernels  72.9 us (32%)
  starting transfers between devices  64 us (28%)
  waiting for transfers between devices  56.4 us (25%)
  between operations  15.7 us (7%)
  local copies, waits for them, and re-layouts  10.3 us (5%)
  other arithmetic  7.63 us (3%)
    pallas_call x4, Pallas kernels, attention(): pl.pallas_call(functools.partial(attend, layout), in_specs=[in_smem] + [a...  70 us
    ppermute x16, starting transfers between devices, swap(): return lax.ppermute(block, 'node', [(i, i ^ mask) for i in range(nodes)])  59.4 us
    ppermute x16, waiting for transfers between devices, swap(): return lax.ppermute(block, 'node', [(i, i ^ mask) for i in range(nodes)])  34.3 us
    all_gather x1, waiting for transfers between devices, local(): blocks = [lax.all_gather(packed, 'node', axis=0, tiled=False)]  19.4 us
    unnamed x32, local copies, waits for them, and re-layouts  7.27 us
  transfers between devices with their start and end apart: 20, of which 11 were waited for; matrix products, arithmetic and copies ran while one was open for 3% of the time, Pallas kernels for 24%

profile of v1, /device:TPU:0, one launch (start us, length us, event | category | flops | bytes accessed | tf_op | source)
XLA Modules:
  0.0 226.9 jit_solution(1839013233777700877)
XLA Ops:
  7.2 0.0 slice-start.1
  7.2 0.0 all-gather.3.cloned.1.call-start
  7.2 0.9 slice.50
  8.2 1.0 slice.51
  9.1 0.8 pad_maximum_fusion.1.refs_1_
  9.9 0.0 all-gather.3.cloned.1.call-update
  10.0 0.0 reduce-scatter.2.cloned.1.call-start
  10.0 3.0 %collective-permute-start = (bf16[128,4096]{1,0:T(8,128)(2,1)}, bf16[128,4096]{1,0:T(8,128)(2,1)S(1)}, u32[]{:S(2)}, u32[]{:S(2)}) collective-permute-start(bf16[128,4096]{1,0:T(8,128)(2,1)} %refs_3_.7), channel_id=1, source_target_pairs={{0,1},{1,0},{2,3},{3,2},{4,5},{5,4},{6,7},{7,6},{8,9},{9,8},{10,11... | collective-permute-start | bytes 3145736 | tf_op jit(solution)/shard_map/ppermute | solution.py:415
  13.1 0.0 copy-start.14
  13.1 1.6 collective-permute-start.1
  14.7 2.6 %collective-permute-start.2 = (bf16[256,256]{1,0:T(8,128)(2,1)S(1)}, bf16[256,256]{1,0:T(8,128)(2,1)S(1)}, u32[]{:S(2)}, u32[]{:S(2)}) collective-permute-start(bf16[256,256]{1,0:T(8,128)(2,1)S(1)} %get-tuple-element.75.refs_1_), channel_id=1, source_target_pairs={{0,16},{2,18},{4,20},{6,22},{8,24},{10,26},{12,28},{14,30},{16,0},... | collective-permute-start | bytes 393224 | tf_op jit(solution)/shard_map/ppermute | solution.py:324
  17.3 0.2 collective-permute-start.3
  17.5 2.0 collective-permute-done.1
  19.6 12.2 %collective-permute-done.2 = bf16[256,256]{1,0:T(8,128)(2,1)S(1)} collective-permute-done((bf16[256,256]{1,0:T(8,128)(2,1)S(1)}, bf16[256,256]{1,0:T(8,128)(2,1)S(1)}, u32[]{:S(2)}, u32[]{:S(2)}) %collective-permute-start.2) | collective-permute-done | bytes 131104 | tf_op jit(solution)/shard_map/ppermute | solution.py:324
  31.8 0.1 pad_maximum_fusion.refs_5_
  31.9 1.8 collective-permute-start.5
  33.7 2.7 %collective-permute-done.refs_4_ = bf16[128,4096]{1,0:T(8,128)(2,1)S(1)} collective-permute-done((bf16[128,4096]{1,0:T(8,128)(2,1)}, bf16[128,4096]{1,0:T(8,128)(2,1)S(1)}, u32[]{:S(2)}, u32[]{:S(2)}) %collective-permute-start) | collective-permute-done | bytes 1048608 | tf_op jit(solution)/shard_map/ppermute | solution.py:415
  36.4 1.0 copy-done.8
  37.4 0.2 copy.17
  37.6 0.5 slice.66
  38.8 2.3 %collective-permute-done.5 = bf16[4,256,256]{2,1,0:T(8,128)(2,1)S(1)} collective-permute-done((bf16[4,256,256]{2,1,0:T(8,128)(2,1)S(1)}, bf16[4,256,256]{2,1,0:T(8,128)(2,1)S(1)}, u32[]{:S(2)}, u32[]{:S(2)}) %collective-permute-start.5) | collective-permute-done | bytes 524320 | tf_op jit(solution)/shard_map/ppermute | solution.py:324
  41.2 0.1 collective-permute-start.6
  41.3 0.7 copy-done.10
  42.0 0.8 copy-done.13
  42.8 0.5 collective-permute-done.6.refs_8_
  43.3 17.1 %shard_map.93 = (bf16[256,4096]{1,0:T(8,128)(2,1)}, f32[256,4096]{1,0:T(8,128)}, f32[256,256]{1,0:T(8,128)}, bf16[16,2,256,256]{3,2,1,0:T(8,128)(2,1)}) custom-call(s32[16]{0:T(128)} %owner_slot.7, bf16[256,4096]{1,0:T(8,128)(2,1)} %refs_0_.7, bf16[256,256]{1,0:T(8,128)(2,1)} %copy-done.14, bf16[4096,4096]{1,0:T(8,128)(2,1)} %refs_2_.7, ...), custom_call_target="tpu_custom_call" | custom-call | flops 36864 | bytes 1048576 | tf_op jit(solution)/shard_map/pallas_call | solution.py:275
  60.5 19.4 %all-gather.3.cloned.1.call-done = bf16[4096,768]{1,0:T(8,128)(2,1)} async-done(((bf16[256,768]{1,0:T(8,128)(2,1)}), bf16[4096,768]{1,0:T(8,128)(2,1)}) %all-gather.3.cloned.1.call-update) | async-done | bytes 6291472 | tf_op jit(solution)/shard_map/all_gather | solution.py:426
  79.8 17.6 %shard_map.94 = (bf16[256,4096]{1,0:T(8,128)(2,1)}, f32[256,4096]{1,0:T(8,128)}, f32[256,256]{1,0:T(8,128)}, bf16[16,2,256,256]{3,2,1,0:T(8,128)(2,1)}) custom-call(s32[16]{0:T(128)} %owner_slot.7, bf16[256,4096]{1,0:T(8,128)(2,1)} %refs_0_.7, ...), custom_call_target="tpu_custom_call", output_to_operand_aliasing={{0}: (7, {}), {1}: (8, {}), {3}: (9, {})} | custom-call | flops 36864 | bytes 1048576 | tf_op jit(solution)/shard_map/pallas_call | solution.py:275
  97.4 0.0 reduce-scatter.2.cloned.1.call-update
  97.5 17.7 %shard_map.95 = (bf16[256,4096]{1,0:T(8,128)(2,1)}, f32[256,4096]{1,0:T(8,128)}, f32[256,256]{1,0:T(8,128)}, bf16[8,256,256]{2,1,0:T(8,128)(2,1)}, bf16[8,256,256]{2,1,0:T(8,128)(2,1)}) custom-call(s32[16]{0:T(128)} %owner_slot.7, bf16[256,4096]{1,0:T(8,128)(2,1)} %refs_0_.7, ...), custom_call_target="tpu_custom_call", output_to_operand_aliasing={{0}: (7, {}), {1}: (8, {})} | custom-call | flops 36864 | bytes 1048576 | tf_op jit(solution)/shard_map/pallas_call | solution.py:275
  115.2 0.1 collective-permute-start.7
  115.2 2.9 %collective-permute-done.7.refs_2_.refs_3_ = bf16[8,256,256]{2,1,0:T(8,128)(2,1)S(1)} collective-permute-done((bf16[8,256,256]{2,1,0:T(8,128)(2,1)}, bf16[8,256,256]{2,1,0:T(8,128)(2,1)S(1)}, u32[]{:S(2)}, u32[]{:S(2)}) %collective-permute-start.7) | collective-permute-done | bytes 1048608 | tf_op jit(solution)/shard_map/ppermute | solution.py:324
  118.1 1.2 copy-done.2
  119.3 1.4 shard_map.96
  120.8 1.0 copy-done.3
  121.8 22.7 %collective-permute-start.8 = (bf16[4,256,256]{2,1,0:T(8,128)(2,1)}, bf16[4,256,256]{2,1,0:T(8,128)(2,1)S(1)}, u32[]{:S(2)}, u32[]{:S(2)}) collective-permute-start(bf16[4,256,256]{2,1,0:T(8,128)(2,1)} %get-tuple-element.45.refs_8_), channel_id=1, source_target_pairs={{0,4},{2,6},{4,0},{6,2},{8,12},{10,14},{12,8},{14,10},{16,20},{18,... | collective-permute-start | bytes 1572872 | tf_op jit(solution)/shard_map/ppermute | solution.py:324
  144.5 17.5 %shard_map.97 = (bf16[256,4096]{1,0:T(8,128)(2,1)}, f32[256,4096]{1,0:T(8,128)}, f32[256,256]{1,0:T(8,128)}, bf16[8,256,256]{2,1,0:T(8,128)(2,1)}, bf16[8,256,256]{2,1,0:T(8,128)(2,1)}) custom-call(s32[16]{0:T(128)} %owner_slot.7, bf16[256,4096]{1,0:T(8,128)(2,1)} %refs_0_.7, ...), custom_call_target="tpu_custom_call", output_to_operand_aliasing={{0}: (7, {}), {1}: (8, {})} | custom-call | flops 36864 | bytes 1048576 | tf_op jit(solution)/shard_map/pallas_call | solution.py:275
  162.0 0.1 collective-permute-start.13
  162.1 0.1 collective-permute-done.8.refs_1_
  162.3 1.2 copy-done.4
  163.5 1.0 copy-done.5
  164.4 0.9 shard_map.98
  165.3 0.1 copy.18
  165.4 0.5 slice.67
  166.6 2.7 %add_convert_fusion.1 = bf16[128,4096]{1,0:T(8,128)(2,1)} fusion(f32[256,4096]{1,0:T(8,128)} %get-tuple-element.46, s32[]{:T(128)S(6)} %select_n.7, f32[]{:T(128)} %bitcast.6), kind=kLoop, calls=%fused_computation.1 | loop fusion | flops 1048576 | bytes 3145736 | tf_op jit(solution)/shard_map/convert_element_type | solution.py:457
  169.3 1.5 collective-permute-start.9
  170.8 0.3 shard_map.99
  171.1 10.5 %collective-permute-start.14 = (bf16[4,256,256]{2,1,0:T(8,128)(2,1)S(1)}, bf16[4,256,256]{2,1,0:T(8,128)(2,1)S(1)}, u32[]{:S(2)}, u32[]{:S(2)}) collective-permute-start(bf16[4,256,256]{2,1,0:T(8,128)(2,1)S(1)} %get-tuple-element.59.refs_2_), channel_id=1, source_target_pairs={{0,4},{2,6},{4,0},{6,2},{8,12},{10,14},{12,8},{14,10},{16,20},{18,... | collective-permute-start | bytes 1572872 | tf_op jit(solution)/shard_map/ppermute | solution.py:324
  181.6 1.8 collective-permute-start.10
  183.4 1.3 collective-permute-start.11
  184.7 1.3 collective-permute-start.12
  186.0 7.5 %collective-permute-done.14.refs_1_ = bf16[4,256,256]{2,1,0:T(8,128)(2,1)S(1)} collective-permute-done((bf16[4,256,256]{2,1,0:T(8,128)(2,1)S(1)}, bf16[4,256,256]{2,1,0:T(8,128)(2,1)S(1)}, u32[]{:S(2)}, u32[]{:S(2)}) %collective-permute-start.14) | collective-permute-done | bytes 524320 | tf_op jit(solution)/shard_map/ppermute | solution.py:324
  193.4 0.2 shard_map.100
  193.7 2.8 %collective-permute-start.15 = (bf16[256,256]{1,0:T(8,128)(2,1)S(1)}, bf16[256,256]{1,0:T(8,128)(2,1)S(1)}, u32[]{:S(2)}, u32[]{:S(2)}) collective-permute-start(bf16[256,256]{1,0:T(8,128)(2,1)S(1)} %get-tuple-element.60.refs_5_), channel_id=1, source_target_pairs={{0,8},{2,10},{4,12},{6,14},{8,0},{10,2},{12,4},{14,6},{16,24},{18,... | collective-permute-start | bytes 393224 | tf_op jit(solution)/shard_map/ppermute | solution.py:324
  196.5 12.4 %collective-permute-start.16 = (bf16[256,256]{1,0:T(8,128)(2,1)S(1)}, bf16[256,256]{1,0:T(8,128)(2,1)S(1)}, u32[]{:S(2)}, u32[]{:S(2)}) collective-permute-start(bf16[256,256]{1,0:T(8,128)(2,1)S(1)} %get-tuple-element.62), channel_id=1, source_target_pairs={{0,16},{2,18},{4,20},{6,22},{8,24},{10,26},{12,28},{14,30},{16,0},... | collective-permute-start | bytes 393224 | tf_op jit(solution)/shard_map/ppermute | solution.py:324
  208.9 2.1 add_convert_fusion.refs_6_
  211.1 0.1 collective-permute-start.17
  211.2 0.1 shard_map.101
  211.3 3.2 %collective-permute-done.16.refs_3_ = bf16[256,256]{1,0:T(8,128)(2,1)S(1)} collective-permute-done((bf16[256,256]{1,0:T(8,128)(2,1)S(1)}, bf16[256,256]{1,0:T(8,128)(2,1)S(1)}, u32[]{:S(2)}, u32[]{:S(2)}) %collective-permute-start.16) | collective-permute-done | bytes 131104 | tf_op jit(solution)/shard_map/ppermute | solution.py:324
  214.5 3.4 %collective-permute-done.17.refs_4_ = bf16[256,256]{1,0:T(8,128)(2,1)S(1)} collective-permute-done((bf16[256,256]{1,0:T(8,128)(2,1)S(1)}, bf16[256,256]{1,0:T(8,128)(2,1)S(1)}, u32[]{:S(2)}, u32[]{:S(2)}) %collective-permute-start.17) | collective-permute-done | bytes 131104 | tf_op jit(solution)/shard_map/ppermute | solution.py:324
  218.0 0.1 shard_map.102
  218.0 0.0 reduce-scatter.2.cloned.1.call-done
  218.1 1.0 fusion.1
  219.2 0.9 pad_maximum_fusion.2
  (40 shorter events, 0.2 us)
Async XLA Ops:
  7.2 5.9 %slice-start = ((bf16[256,512]{1,0:T(8,128)(2,1)}), bf16[256,128]{1,0:T(8,128)(2,1)S(1)}, s32[]{:S(2)}) async-start(bf16[256,512]{1,0:T(8,128)(2,1)} %param.7), calls=%async_computation.3 | async-start | bytes 131072 | tf_op jit(solution)/shard_map/slice | solution.py:422
  7.2 5.9 %slice-start.1 = ((bf16[256,512]{1,0:T(8,128)(2,1)}), bf16[256,128]{1,0:T(8,128)(2,1)S(1)}, s32[]{:S(2)}) async-start(bf16[256,512]{1,0:T(8,128)(2,1)} %param.8), calls=%async_computation.4 | async-start | bytes 131072 | tf_op jit(solution)/shard_map/slice | solution.py:422
  7.2 72.6 %all-gather.3.cloned.1.call-start = ((), (), s32[]{:S(2)}) async-start(), calls=%async_computation.2 | async-start | bytes 6684672 | tf_op jit(solution)/shard_map/all_gather | solution.py:426
  10.0 208.1 %reduce-scatter.2.cloned.1.call-start = ((), (), s32[]{:S(2)}) async-start(), calls=%async_computation.1 | async-start | bytes 4456448 | tf_op jit(solution)/shard_map/reduce_scatter | solution.py:443
  10.0 26.4 %collective-permute-start = (bf16[128,4096]{1,0:T(8,128)(2,1)}, bf16[128,4096]{1,0:T(8,128)(2,1)S(1)}, u32[]{:S(2)}, u32[]{:S(2)}) collective-permute-start(bf16[128,4096]{1,0:T(8,128)(2,1)} %refs_3_.7), channel_id=1, source_target_pairs={{0,1},{1,0},{2,3},{3,2},{4,5},{5,4},{6,7},{7,6},{8,9},{9,8},{10,11... | collective-permute-start | bytes 3145736 | tf_op jit(solution)/shard_map/ppermute | solution.py:415
  13.1 28.1 %copy-start.14 = (bf16[256,256]{1,0:T(8,128)(2,1)}, bf16[256,256]{1,0:T(8,128)(2,1)S(1)}, u32[]{:S(2)}) copy-start(bf16[256,256]{1,0:T(8,128)(2,1)S(1)} %get-tuple-element.75.refs_1_) | copy-start | bytes 393220
  13.1 6.5 %collective-permute-start.1 = (bf16[256,256]{1,0:T(8,128)(2,1)S(1)}, bf16[256,256]{1,0:T(8,128)(2,1)S(1)}, u32[]{:S(2)}, u32[]{:S(2)}) collective-permute-start(bf16[256,256]{1,0:T(8,128)(2,1)S(1)} %get-tuple-element.75.refs_1_), channel_id=1, source_target_pairs={{0,8},{2,10},{4,12},{6,14},{8,0},{10,2},{12,4},{14,6},{16,24},{18,... | collective-permute-start | bytes 393224 | tf_op jit(solution)/shard_map/ppermute | solution.py:324
  14.7 17.1 %collective-permute-start.2 = (bf16[256,256]{1,0:T(8,128)(2,1)S(1)}, bf16[256,256]{1,0:T(8,128)(2,1)S(1)}, u32[]{:S(2)}, u32[]{:S(2)}) collective-permute-start(bf16[256,256]{1,0:T(8,128)(2,1)S(1)} %get-tuple-element.75.refs_1_), channel_id=1, source_target_pairs={{0,16},{2,18},{4,20},{6,22},{8,24},{10,26},{12,28},{14,30},{16,0},... | collective-permute-start | bytes 393224 | tf_op jit(solution)/shard_map/ppermute | solution.py:324
  17.3 14.5 %collective-permute-start.3 = (bf16[256,256]{1,0:T(8,128)(2,1)S(1)}, bf16[256,256]{1,0:T(8,128)(2,1)S(1)}, u32[]{:S(2)}, u32[]{:S(2)}) collective-permute-start(bf16[256,256]{1,0:T(8,128)(2,1)S(1)} %get-tuple-element.75.refs_1_), channel_id=1, source_target_pairs={{0,24},{2,26},{4,28},{6,30},{8,16},{10,18},{12,20},{14,22},{16,8},... | collective-permute-start | bytes 393224 | tf_op jit(solution)/shard_map/ppermute | solution.py:324
  31.9 11.4 %copy-start.9 = (bf16[4,256,256]{2,1,0:T(8,128)(2,1)}, bf16[4,256,256]{2,1,0:T(8,128)(2,1)S(1)}, u32[]{:S(2)}) copy-start(bf16[4,256,256]{2,1,0:T(8,128)(2,1)S(1)} %pad_maximum_fusion.refs_5_) | copy-start | bytes 1572868
  31.9 9.2 %collective-permute-start.5 = (bf16[4,256,256]{2,1,0:T(8,128)(2,1)S(1)}, bf16[4,256,256]{2,1,0:T(8,128)(2,1)S(1)}, u32[]{:S(2)}, u32[]{:S(2)}) collective-permute-start(bf16[4,256,256]{2,1,0:T(8,128)(2,1)S(1)} %pad_maximum_fusion.refs_5_), channel_id=1, source_target_pairs={{0,4},{2,6},{4,0},{6,2},{8,12},{10,14},{12,8},{14,10},{16,20},{18,... | collective-permute-start | bytes 1572872 | tf_op jit(solution)/shard_map/ppermute | solution.py:324
  33.7 7.6 %collective-permute-start.4 = (bf16[4,256,256]{2,1,0:T(8,128)(2,1)S(1)}, bf16[4,256,256]{2,1,0:T(8,128)(2,1)S(1)}, u32[]{:S(2)}, u32[]{:S(2)}) collective-permute-start(bf16[4,256,256]{2,1,0:T(8,128)(2,1)S(1)} %pad_maximum_fusion.refs_5_), channel_id=1, source_target_pairs={{0,2},{2,0},{4,6},{6,4},{8,10},{10,8},{12,14},{14,12},{16,18},{18,... | collective-permute-start | bytes 1572872 | tf_op jit(solution)/shard_map/ppermute | solution.py:324
  36.4 1.0 copy-start.8
  41.2 0.8 copy-start.10
  41.2 2.1 collective-permute-start.6
  42.0 0.8 copy-start.13
  115.2 2.9 %collective-permute-start.7 = (bf16[8,256,256]{2,1,0:T(8,128)(2,1)}, bf16[8,256,256]{2,1,0:T(8,128)(2,1)S(1)}, u32[]{:S(2)}, u32[]{:S(2)}) collective-permute-start(bf16[8,256,256]{2,1,0:T(8,128)(2,1)} %get-tuple-element.44), channel_id=1, source_target_pairs={{0,2},{2,0},{4,6},{6,4},{8,10},{10,8},{12,14},{14,12},{16,18},{18,... | collective-permute-start | bytes 3145736 | tf_op jit(solution)/shard_map/ppermute | solution.py:324
  118.1 1.2 copy-start.2
  120.8 1.0 copy-start.3
  121.8 40.5 %collective-permute-start.8 = (bf16[4,256,256]{2,1,0:T(8,128)(2,1)}, bf16[4,256,256]{2,1,0:T(8,128)(2,1)S(1)}, u32[]{:S(2)}, u32[]{:S(2)}) collective-permute-start(bf16[4,256,256]{2,1,0:T(8,128)(2,1)} %get-tuple-element.45.refs_8_), channel_id=1, source_target_pairs={{0,4},{2,6},{4,0},{6,2},{8,12},{10,14},{12,8},{14,10},{16,20},{18,... | collective-permute-start | bytes 1572872 | tf_op jit(solution)/shard_map/ppermute | solution.py:324
  162.0 8.7 %collective-permute-start.13 = (bf16[8,256,256]{2,1,0:T(8,128)(2,1)}, bf16[8,256,256]{2,1,0:T(8,128)(2,1)S(1)}, u32[]{:S(2)}, u32[]{:S(2)}) collective-permute-start(bf16[8,256,256]{2,1,0:T(8,128)(2,1)} %get-tuple-element.57), channel_id=1, source_target_pairs={{0,2},{2,0},{4,6},{6,4},{8,10},{10,8},{12,14},{14,12},{16,18},{18,... | collective-permute-start | bytes 3145736 | tf_op jit(solution)/shard_map/ppermute | solution.py:324
  162.3 1.2 copy-start.4
  163.5 1.0 copy-start.5
  165.3 5.5 %copy-start.1 = (bf16[8,256,256]{2,1,0:T(8,128)(2,1)S(1)}, bf16[8,256,256]{2,1,0:T(8,128)(2,1)}, u32[]{:S(2)}) copy-start(bf16[8,256,256]{2,1,0:T(8,128)(2,1)} %get-tuple-element.56.refs_0_.refs_1_) | copy-start | bytes 3145732
  169.3 27.2 %collective-permute-start.9 = (bf16[128,4096]{1,0:T(8,128)(2,1)}, bf16[128,4096]{1,0:T(8,128)(2,1)}, u32[]{:S(2)}, u32[]{:S(2)}) collective-permute-start(bf16[128,4096]{1,0:T(8,128)(2,1)} %add_convert_fusion.1), channel_id=1, source_target_pairs={{0,1},{1,0},{2,3},{3,2},{4,5},{5,4},{6,7},{7,6},{8,9},{9,8},{10,11... | collective-permute-start | bytes 3145736 | tf_op jit(solution)/shard_map/ppermute | solution.py:459
  171.1 22.4 %collective-permute-start.14 = (bf16[4,256,256]{2,1,0:T(8,128)(2,1)S(1)}, bf16[4,256,256]{2,1,0:T(8,128)(2,1)S(1)}, u32[]{:S(2)}, u32[]{:S(2)}) collective-permute-start(bf16[4,256,256]{2,1,0:T(8,128)(2,1)S(1)} %get-tuple-element.59.refs_2_), channel_id=1, source_target_pairs={{0,4},{2,6},{4,0},{6,2},{8,12},{10,14},{12,8},{14,10},{16,20},{18,... | collective-permute-start | bytes 1572872 | tf_op jit(solution)/shard_map/ppermute | solution.py:324
  181.6 29.5 %collective-permute-start.10 = (bf16[256,256]{1,0:T(8,128)(2,1)S(1)}, bf16[256,256]{1,0:T(8,128)(2,1)S(1)}, u32[]{:S(2)}, u32[]{:S(2)}) collective-permute-start(bf16[256,256]{1,0:T(8,128)(2,1)S(1)} %get-tuple-element.49.refs_4_), channel_id=1, source_target_pairs={{0,8},{2,10},{4,12},{6,14},{8,0},{10,2},{12,4},{14,6},{16,24},{18,... | collective-permute-start | bytes 393224 | tf_op jit(solution)/shard_map/ppermute | solution.py:324
  183.4 27.7 %collective-permute-start.11 = (bf16[256,256]{1,0:T(8,128)(2,1)}, bf16[256,256]{1,0:T(8,128)(2,1)S(1)}, u32[]{:S(2)}, u32[]{:S(2)}) collective-permute-start(bf16[256,256]{1,0:T(8,128)(2,1)} %get-tuple-element.54), channel_id=1, source_target_pairs={{0,16},{2,18},{4,20},{6,22},{8,24},{10,26},{12,28},{14,30},{16,0},... | collective-permute-start | bytes 393224 | tf_op jit(solution)/shard_map/ppermute | solution.py:324
  184.7 26.5 %collective-permute-start.12 = (bf16[256,256]{1,0:T(8,128)(2,1)S(1)}, bf16[256,256]{1,0:T(8,128)(2,1)S(1)}, u32[]{:S(2)}, u32[]{:S(2)}) collective-permute-start(bf16[256,256]{1,0:T(8,128)(2,1)S(1)} %get-tuple-element.55), channel_id=1, source_target_pairs={{0,24},{2,26},{4,28},{6,30},{8,16},{10,18},{12,20},{14,22},{16,8},... | collective-permute-start | bytes 393224 | tf_op jit(solution)/shard_map/ppermute | solution.py:324
  193.7 17.6 %collective-permute-start.15 = (bf16[256,256]{1,0:T(8,128)(2,1)S(1)}, bf16[256,256]{1,0:T(8,128)(2,1)S(1)}, u32[]{:S(2)}, u32[]{:S(2)}) collective-permute-start(bf16[256,256]{1,0:T(8,128)(2,1)S(1)} %get-tuple-element.60.refs_5_), channel_id=1, source_target_pairs={{0,8},{2,10},{4,12},{6,14},{8,0},{10,2},{12,4},{14,6},{16,24},{18,... | collective-permute-start | bytes 393224 | tf_op jit(solution)/shard_map/ppermute | solution.py:324
  196.5 14.7 %copy-start.7 = (f32[256,256]{1,0:T(8,128)S(1)}, f32[256,256]{1,0:T(8,128)}, u32[]{:S(2)}) copy-start(f32[256,256]{1,0:T(8,128)} %get-tuple-element.52.refs_0_) | copy-start | bytes 786436
  196.5 18.0 %collective-permute-start.16 = (bf16[256,256]{1,0:T(8,128)(2,1)S(1)}, bf16[256,256]{1,0:T(8,128)(2,1)S(1)}, u32[]{:S(2)}, u32[]{:S(2)}) collective-permute-start(bf16[256,256]{1,0:T(8,128)(2,1)S(1)} %get-tuple-element.62), channel_id=1, source_target_pairs={{0,16},{2,18},{4,20},{6,22},{8,24},{10,26},{12,28},{14,30},{16,0},... | collective-permute-start | bytes 393224 | tf_op jit(solution)/shard_map/ppermute | solution.py:324
  211.0 8.1 %copy-start = (bf16[128,4096]{1,0:T(8,128)(2,1)}, bf16[128,4096]{1,0:T(8,128)(2,1)S(1)}, u32[]{:S(2)}) copy-start(bf16[128,4096]{1,0:T(8,128)(2,1)S(1)} %add_convert_fusion.refs_6_) | copy-start | bytes 3145732
  211.0 6.9 %copy-start.6 = (f32[256,256]{1,0:T(8,128)S(1)}, f32[256,256]{1,0:T(8,128)}, u32[]{:S(2)}) copy-start(f32[256,256]{1,0:T(8,128)} %get-tuple-element.48.refs_2_.refs_0_) | copy-start | bytes 786436
  211.0 7.0 %copy-start.11 = (f32[256,256]{1,0:T(8,128)S(1)}, f32[256,256]{1,0:T(8,128)}, u32[]{:S(2)}) copy-start(f32[256,256]{1,0:T(8,128)} %get-tuple-element.37.refs_9_) | copy-start | bytes 786436
  211.0 7.0 %copy-start.12 = (f32[256,256]{1,0:T(8,128)S(1)}, f32[256,256]{1,0:T(8,128)}, u32[]{:S(2)}) copy-start(f32[256,256]{1,0:T(8,128)} %get-tuple-element.40.refs_8_) | copy-start | bytes 786436
  211.1 6.9 %collective-permute-start.17 = (bf16[256,256]{1,0:T(8,128)(2,1)S(1)}, bf16[256,256]{1,0:T(8,128)(2,1)S(1)}, u32[]{:S(2)}, u32[]{:S(2)}) collective-permute-start(bf16[256,256]{1,0:T(8,128)(2,1)S(1)} %get-tuple-element.63), channel_id=1, source_target_pairs={{0,24},{2,26},{4,28},{6,30},{8,16},{10,18},{12,20},{14,22},{16,8},... | collective-permute-start | bytes 393224 | tf_op jit(solution)/shard_map/ppermute | solution.py:324
Sparse Core Ops, SparseCore 0:
  10.3 69.4 all-gather.2
  97.6 89.2 reduce-scatter.1

commit v2 on v1

--- a/solution.py
+++ b/solution.py
@@ -464,7 +464,7 @@
     totals = []
     for chain in earlier + [last]:
         try:
-            chain.send([moved] if chain is last else [moved, projected])
+            chain.send([moved])
         except StopIteration as end:
             totals.append(end.value)
     if offloaded:

time: 228 us -> 221 us (0.969)
  Pallas kernels: 72.9 us -> 117 us
  starting transfers between devices: 64 us -> 24 us
  waiting for transfers between devices: 56.4 us -> 44 us
    pallas_call x4, Pallas kernels: 70 us -> 114 us  [attention(): pl.pallas_call(functools.partial(attend, layout), in_specs=[in_smem] + [a...]
    ppermute x16, starting transfers between devices: 59.4 us -> 20.1 us  [swap(): return lax.ppermute(block, 'node', [(i, i ^ mask) for i in range(nodes)])]
    all_gather x1, waiting for transfers between devices: 19.4 us -> 7.96 us  [local(): blocks = [lax.all_gather(packed, 'node', axis=0, tiled=False)]]
    ppermute x16, waiting for transfers between devices: 34.3 us -> 29.6 us  [swap(): return lax.ppermute(block, 'node', [(i, i ^ mask) for i in range(nodes)])]
    ppermute x1, waiting for transfers between devices: 0.01 us -> 3.6 us  [local(): projected = here + lax.ppermute(away, 'tp', [(0, 1), (1, 0)]).astype(f32)]
    unnamed x32 -> x30, local copies, waits for them, and re-layouts: 7.27 us -> 7.33 us
  transfers between devices with their start and end apart: 20 -> 20, of which waited for: 11 -> 10; matrix products, arithmetic and copies ran while one was open for 3% -> 3% of each run, Pallas kernels for 24% -> 40%
where the time goes in v2:
time: 221 us; the launch traced here: 220 us
  Pallas kernels  117 us (53%)
  waiting for transfers between devices  44 us (20%)
  starting transfers between devices  24 us (11%)
  between operations  15.7 us (7%)
  local copies, waits for them, and re-layouts  10.3 us (5%)
  other arithmetic  8.69 us (4%)
    pallas_call x4, Pallas kernels, attention(): pl.pallas_call(functools.partial(attend, layout), in_specs=[in_smem] + [a...  114 us
    ppermute x16, waiting for transfers between devices, swap(): return lax.ppermute(block, 'node', [(i, i ^ mask) for i in range(nodes)])  29.6 us
    ppermute x16, starting transfers between devices, swap(): return lax.ppermute(block, 'node', [(i, i ^ mask) for i in range(nodes)])  20.1 us
    all_gather x1, waiting for transfers between devices, local(): blocks = [lax.all_gather(packed, 'node', axis=0, tiled=False)]  7.96 us
    unnamed x30, local copies, waits for them, and re-layouts  7.33 us
  transfers between devices with their start and end apart: 20, of which 10 were waited for; matrix products, arithmetic and copies ran while one was open for 3% of the time, Pallas kernels for 40%

profile of v2, /device:TPU:0, one launch (start us, length us, event | category | flops | bytes accessed | tf_op | source)
XLA Modules:
  0.0 219.8 jit_solution(11169112681119787005)
XLA Ops:
  7.2 0.0 slice-start.1
  7.2 0.0 all-gather.3.cloned.1.call-start
  7.2 0.9 slice.50
  8.2 1.0 slice.51
  9.1 0.8 pad_maximum_fusion.1.refs_1_
  9.9 0.0 all-gather.3.cloned.1.call-update
  10.0 0.0 reduce-scatter.2.cloned.1.call-start
  10.0 3.0 %collective-permute-start = (bf16[128,4096]{1,0:T(8,128)(2,1)}, bf16[128,4096]{1,0:T(8,128)(2,1)S(1)}, u32[]{:S(2)}, u32[]{:S(2)}) collective-permute-start(bf16[128,4096]{1,0:T(8,128)(2,1)} %refs_3_.7), channel_id=1, source_target_pairs={{0,1},{1,0},{2,3},{3,2},{4,5},{5,4},{6,7},{7,6},{8,9},{9,8},{10,11... | collective-permute-start | bytes 3145736 | tf_op jit(solution)/shard_map/ppermute | solution.py:415
  13.1 0.0 copy-start.13
  13.1 1.6 collective-permute-start.1
  14.7 2.6 %collective-permute-start.2 = (bf16[256,256]{1,0:T(8,128)(2,1)S(1)}, bf16[256,256]{1,0:T(8,128)(2,1)S(1)}, u32[]{:S(2)}, u32[]{:S(2)}) collective-permute-start(bf16[256,256]{1,0:T(8,128)(2,1)S(1)} %get-tuple-element.75.refs_1_), channel_id=1, source_target_pairs={{0,16},{2,18},{4,20},{6,22},{8,24},{10,26},{12,28},{14,30},{16,0},... | collective-permute-start | bytes 393224 | tf_op jit(solution)/shard_map/ppermute | solution.py:324
  17.3 0.2 collective-permute-start.3
  17.5 2.0 collective-permute-done.1
  19.6 12.2 %collective-permute-done.2 = bf16[256,256]{1,0:T(8,128)(2,1)S(1)} collective-permute-done((bf16[256,256]{1,0:T(8,128)(2,1)S(1)}, bf16[256,256]{1,0:T(8,128)(2,1)S(1)}, u32[]{:S(2)}, u32[]{:S(2)}) %collective-permute-start.2) | collective-permute-done | bytes 131104 | tf_op jit(solution)/shard_map/ppermute | solution.py:324
  31.8 0.1 pad_maximum_fusion.refs_5_
  31.9 1.8 collective-permute-start.5
  33.7 2.7 %collective-permute-done.refs_4_ = bf16[128,4096]{1,0:T(8,128)(2,1)S(1)} collective-permute-done((bf16[128,4096]{1,0:T(8,128)(2,1)}, bf16[128,4096]{1,0:T(8,128)(2,1)S(1)}, u32[]{:S(2)}, u32[]{:S(2)}) %collective-permute-start) | collective-permute-done | bytes 1048608 | tf_op jit(solution)/shard_map/ppermute | solution.py:415
  36.4 1.0 copy-done.7
  37.4 0.2 copy.17
  37.6 0.5 slice.66
  38.8 2.3 %collective-permute-done.5 = bf16[4,256,256]{2,1,0:T(8,128)(2,1)S(1)} collective-permute-done((bf16[4,256,256]{2,1,0:T(8,128)(2,1)S(1)}, bf16[4,256,256]{2,1,0:T(8,128)(2,1)S(1)}, u32[]{:S(2)}, u32[]{:S(2)}) %collective-permute-start.5) | collective-permute-done | bytes 524320 | tf_op jit(solution)/shard_map/ppermute | solution.py:324
  41.2 0.1 collective-permute-start.6
  41.3 0.7 copy-done.9
  42.0 0.8 copy-done.12
  42.8 0.5 collective-permute-done.6.refs_8_
  43.3 28.5 %shard_map.93 = (bf16[256,4096]{1,0:T(8,128)(2,1)}, f32[256,4096]{1,0:T(8,128)}, f32[256,256]{1,0:T(8,128)}, bf16[16,2,256,256]{3,2,1,0:T(8,128)(2,1)}) custom-call(s32[16]{0:T(128)} %owner_slot.7, bf16[256,4096]{1,0:T(8,128)(2,1)} %refs_0_.7, bf16[256,256]{1,0:T(8,128)(2,1)} %copy-done.13, bf16[4096,4096]{1,0:T(8,128)(2,1)} %refs_2_.7, ...), custom_call_target="tpu_custom_call" | custom-call | flops 36864 | bytes 1048576 | tf_op jit(solution)/shard_map/pallas_call | solution.py:275
  71.8 8.0 %all-gather.3.cloned.1.call-done = bf16[4096,768]{1,0:T(8,128)(2,1)} async-done(((bf16[256,768]{1,0:T(8,128)(2,1)}), bf16[4096,768]{1,0:T(8,128)(2,1)}) %all-gather.3.cloned.1.call-update) | async-done | bytes 6291472 | tf_op jit(solution)/shard_map/all_gather | solution.py:426
  79.8 28.7 %shard_map.94 = (bf16[256,4096]{1,0:T(8,128)(2,1)}, f32[256,4096]{1,0:T(8,128)}, f32[256,256]{1,0:T(8,128)}, bf16[16,2,256,256]{3,2,1,0:T(8,128)(2,1)}) custom-call(s32[16]{0:T(128)} %owner_slot.7, bf16[256,4096]{1,0:T(8,128)(2,1)} %refs_0_.7, ...), custom_call_target="tpu_custom_call", output_to_operand_aliasing={{0}: (7, {}), {1}: (8, {}), {3}: (9, {})} | custom-call | flops 36864 | bytes 1048576 | tf_op jit(solution)/shard_map/pallas_call | solution.py:275
  108.5 0.0 reduce-scatter.2.cloned.1.call-update
  108.5 28.6 %shard_map.95 = (bf16[256,4096]{1,0:T(8,128)(2,1)}, f32[256,4096]{1,0:T(8,128)}, f32[256,256]{1,0:T(8,128)}, bf16[8,256,256]{2,1,0:T(8,128)(2,1)}, bf16[8,256,256]{2,1,0:T(8,128)(2,1)}) custom-call(s32[16]{0:T(128)} %owner_slot.7, bf16[256,4096]{1,0:T(8,128)(2,1)} %refs_0_.7, ...), custom_call_target="tpu_custom_call", output_to_operand_aliasing={{0}: (7, {}), {1}: (8, {})} | custom-call | flops 36864 | bytes 1048576 | tf_op jit(solution)/shard_map/pallas_call | solution.py:275
  137.1 0.1 collective-permute-start.7
  137.2 2.9 %collective-permute-done.7.refs_2_.refs_3_ = bf16[8,256,256]{2,1,0:T(8,128)(2,1)S(1)} collective-permute-done((bf16[8,256,256]{2,1,0:T(8,128)(2,1)}, bf16[8,256,256]{2,1,0:T(8,128)(2,1)S(1)}, u32[]{:S(2)}, u32[]{:S(2)}) %collective-permute-start.7) | collective-permute-done | bytes 1048608 | tf_op jit(solution)/shard_map/ppermute | solution.py:324
  140.0 1.3 copy-done.1
  141.4 1.5 shard_map.96
  142.8 1.0 copy-done.2
  143.8 0.9 collective-permute-start.8
  144.7 28.4 %shard_map.97 = (bf16[256,4096]{1,0:T(8,128)(2,1)}, f32[256,4096]{1,0:T(8,128)}, f32[256,256]{1,0:T(8,128)}, bf16[8,256,256]{2,1,0:T(8,128)(2,1)}, bf16[8,256,256]{2,1,0:T(8,128)(2,1)}) custom-call(s32[16]{0:T(128)} %owner_slot.7, bf16[256,4096]{1,0:T(8,128)(2,1)} %refs_0_.7, ...), custom_call_target="tpu_custom_call", output_to_operand_aliasing={{0}: (7, {}), {1}: (8, {})} | custom-call | flops 36864 | bytes 1048576 | tf_op jit(solution)/shard_map/pallas_call | solution.py:275
  173.1 0.1 collective-permute-start.13
  173.2 1.2 copy-done.3
  174.4 0.9 copy-done.4
  175.4 0.9 shard_map.98
  176.3 0.1 copy.18
  176.4 0.5 slice.67
  177.6 2.8 %add_convert_fusion.1 = bf16[128,4096]{1,0:T(8,128)(2,1)} fusion(f32[256,4096]{1,0:T(8,128)} %get-tuple-element.46, s32[]{:T(128)S(6)} %select_n.7, f32[]{:T(128)} %bitcast.6), kind=kLoop, calls=%fused_computation.1 | loop fusion | flops 1048576 | bytes 3145736 | tf_op jit(solution)/shard_map/convert_element_type | solution.py:457
  180.3 0.7 collective-permute-start.9
  181.1 0.3 shard_map.99
  181.4 0.6 collective-permute-start.14
  182.0 0.2 collective-permute-start.10
  182.2 3.8 %collective-permute-start.11 = (bf16[256,256]{1,0:T(8,128)(2,1)}, bf16[256,256]{1,0:T(8,128)(2,1)S(1)}, u32[]{:S(2)}, u32[]{:S(2)}) collective-permute-start(bf16[256,256]{1,0:T(8,128)(2,1)} %get-tuple-element.54), channel_id=1, source_target_pairs={{0,16},{2,18},{4,20},{6,22},{8,24},{10,26},{12,28},{14,30},{16,0},... | collective-permute-start | bytes 393224 | tf_op jit(solution)/shard_map/ppermute | solution.py:324
  186.0 1.5 collective-permute-start.12
  187.5 8.1 %collective-permute-done.14.refs_1_ = bf16[4,256,256]{2,1,0:T(8,128)(2,1)S(1)} collective-permute-done((bf16[4,256,256]{2,1,0:T(8,128)(2,1)S(1)}, bf16[4,256,256]{2,1,0:T(8,128)(2,1)S(1)}, u32[]{:S(2)}, u32[]{:S(2)}) %collective-permute-start.14) | collective-permute-done | bytes 524320 | tf_op jit(solution)/shard_map/ppermute | solution.py:324
  195.6 0.2 shard_map.100
  195.8 0.2 collective-permute-start.15
  196.0 4.3 %collective-permute-start.16 = (bf16[256,256]{1,0:T(8,128)(2,1)S(1)}, bf16[256,256]{1,0:T(8,128)(2,1)S(1)}, u32[]{:S(2)}, u32[]{:S(2)}) collective-permute-start(bf16[256,256]{1,0:T(8,128)(2,1)S(1)} %get-tuple-element.62), channel_id=1, source_target_pairs={{0,16},{2,18},{4,20},{6,22},{8,24},{10,26},{12,28},{14,30},{16,0},... | collective-permute-start | bytes 393224 | tf_op jit(solution)/shard_map/ppermute | solution.py:324
  200.4 2.1 collective-permute-start.17
  202.5 0.1 shard_map.101
  202.6 0.0 copy-start.10
  202.6 3.6 %collective-permute-done.9 = bf16[128,4096]{1,0:T(8,128)(2,1)} collective-permute-done((bf16[128,4096]{1,0:T(8,128)(2,1)}, bf16[128,4096]{1,0:T(8,128)(2,1)}, u32[]{:S(2)}, u32[]{:S(2)}) %collective-permute-start.9) | collective-permute-done | bytes 1048608 | tf_op jit(solution)/shard_map/ppermute | solution.py:459
  206.2 3.1 %add_convert_fusion = bf16[128,4096]{1,0:T(8,128)(2,1)} fusion(bf16[128,4096]{1,0:T(8,128)(2,1)} %collective-permute-done.9, f32[256,4096]{1,0:T(8,128)} %get-tuple-element.46, s32[]{:T(128)S(6)} %select_n.6), kind=kLoop, calls=%fused_computation | loop fusion | flops 1572864 | bytes 4194308 | tf_op jit(solution)/shard_map/convert_element_type | solution.py:460
  209.3 1.5 collective-permute-done.16.refs_3_
  210.9 0.1 shard_map.102
  211.0 0.0 reduce-scatter.2.cloned.1.call-done
  211.0 1.0 fusion.1
  212.1 0.9 pad_maximum_fusion.2
  (38 shorter events, 0.2 us)
Async XLA Ops:
  7.2 5.9 %slice-start = ((bf16[256,512]{1,0:T(8,128)(2,1)}), bf16[256,128]{1,0:T(8,128)(2,1)S(1)}, s32[]{:S(2)}) async-start(bf16[256,512]{1,0:T(8,128)(2,1)} %param.7), calls=%async_computation.3 | async-start | bytes 131072 | tf_op jit(solution)/shard_map/slice | solution.py:422
  7.2 5.9 %slice-start.1 = ((bf16[256,512]{1,0:T(8,128)(2,1)}), bf16[256,128]{1,0:T(8,128)(2,1)S(1)}, s32[]{:S(2)}) async-start(bf16[256,512]{1,0:T(8,128)(2,1)} %param.8), calls=%async_computation.4 | async-start | bytes 131072 | tf_op jit(solution)/shard_map/slice | solution.py:422
  7.2 72.6 %all-gather.3.cloned.1.call-start = ((), (), s32[]{:S(2)}) async-start(), calls=%async_computation.2 | async-start | bytes 6684672 | tf_op jit(solution)/shard_map/all_gather | solution.py:426
  10.0 201.0 %reduce-scatter.2.cloned.1.call-start = ((), (), s32[]{:S(2)}) async-start(), calls=%async_computation.1 | async-start | bytes 4456448 | tf_op jit(solution)/shard_map/reduce_scatter | solution.py:443
  10.0 26.4 %collective-permute-start = (bf16[128,4096]{1,0:T(8,128)(2,1)}, bf16[128,4096]{1,0:T(8,128)(2,1)S(1)}, u32[]{:S(2)}, u32[]{:S(2)}) collective-permute-start(bf16[128,4096]{1,0:T(8,128)(2,1)} %refs_3_.7), channel_id=1, source_target_pairs={{0,1},{1,0},{2,3},{3,2},{4,5},{5,4},{6,7},{7,6},{8,9},{9,8},{10,11... | collective-permute-start | bytes 3145736 | tf_op jit(solution)/shard_map/ppermute | solution.py:415
  13.1 28.1 %copy-start.13 = (bf16[256,256]{1,0:T(8,128)(2,1)}, bf16[256,256]{1,0:T(8,128)(2,1)S(1)}, u32[]{:S(2)}) copy-start(bf16[256,256]{1,0:T(8,128)(2,1)S(1)} %get-tuple-element.75.refs_1_) | copy-start | bytes 393220
  13.1 6.5 %collective-permute-start.1 = (bf16[256,256]{1,0:T(8,128)(2,1)S(1)}, bf16[256,256]{1,0:T(8,128)(2,1)S(1)}, u32[]{:S(2)}, u32[]{:S(2)}) collective-permute-start(bf16[256,256]{1,0:T(8,128)(2,1)S(1)} %get-tuple-element.75.refs_1_), channel_id=1, source_target_pairs={{0,8},{2,10},{4,12},{6,14},{8,0},{10,2},{12,4},{14,6},{16,24},{18,... | collective-permute-start | bytes 393224 | tf_op jit(solution)/shard_map/ppermute | solution.py:324
  14.7 17.1 %collective-permute-start.2 = (bf16[256,256]{1,0:T(8,128)(2,1)S(1)}, bf16[256,256]{1,0:T(8,128)(2,1)S(1)}, u32[]{:S(2)}, u32[]{:S(2)}) collective-permute-start(bf16[256,256]{1,0:T(8,128)(2,1)S(1)} %get-tuple-element.75.refs_1_), channel_id=1, source_target_pairs={{0,16},{2,18},{4,20},{6,22},{8,24},{10,26},{12,28},{14,30},{16,0},... | collective-permute-start | bytes 393224 | tf_op jit(solution)/shard_map/ppermute | solution.py:324
  17.3 14.5 %collective-permute-start.3 = (bf16[256,256]{1,0:T(8,128)(2,1)S(1)}, bf16[256,256]{1,0:T(8,128)(2,1)S(1)}, u32[]{:S(2)}, u32[]{:S(2)}) collective-permute-start(bf16[256,256]{1,0:T(8,128)(2,1)S(1)} %get-tuple-element.75.refs_1_), channel_id=1, source_target_pairs={{0,24},{2,26},{4,28},{6,30},{8,16},{10,18},{12,20},{14,22},{16,8},... | collective-permute-start | bytes 393224 | tf_op jit(solution)/shard_map/ppermute | solution.py:324
  31.9 11.4 %copy-start.8 = (bf16[4,256,256]{2,1,0:T(8,128)(2,1)}, bf16[4,256,256]{2,1,0:T(8,128)(2,1)S(1)}, u32[]{:S(2)}) copy-start(bf16[4,256,256]{2,1,0:T(8,128)(2,1)S(1)} %pad_maximum_fusion.refs_5_) | copy-start | bytes 1572868
  31.9 9.2 %collective-permute-start.5 = (bf16[4,256,256]{2,1,0:T(8,128)(2,1)S(1)}, bf16[4,256,256]{2,1,0:T(8,128)(2,1)S(1)}, u32[]{:S(2)}, u32[]{:S(2)}) collective-permute-start(bf16[4,256,256]{2,1,0:T(8,128)(2,1)S(1)} %pad_maximum_fusion.refs_5_), channel_id=1, source_target_pairs={{0,4},{2,6},{4,0},{6,2},{8,12},{10,14},{12,8},{14,10},{16,20},{18,... | collective-permute-start | bytes 1572872 | tf_op jit(solution)/shard_map/ppermute | solution.py:324
  33.7 7.6 %collective-permute-start.4 = (bf16[4,256,256]{2,1,0:T(8,128)(2,1)S(1)}, bf16[4,256,256]{2,1,0:T(8,128)(2,1)S(1)}, u32[]{:S(2)}, u32[]{:S(2)}) collective-permute-start(bf16[4,256,256]{2,1,0:T(8,128)(2,1)S(1)} %pad_maximum_fusion.refs_5_), channel_id=1, source_target_pairs={{0,2},{2,0},{4,6},{6,4},{8,10},{10,8},{12,14},{14,12},{16,18},{18,... | collective-permute-start | bytes 1572872 | tf_op jit(solution)/shard_map/ppermute | solution.py:324
  36.4 1.0 copy-start.7
  41.2 0.8 copy-start.9
  41.2 2.1 collective-permute-start.6
  42.0 0.8 copy-start.12
  137.1 2.9 %collective-permute-start.7 = (bf16[8,256,256]{2,1,0:T(8,128)(2,1)}, bf16[8,256,256]{2,1,0:T(8,128)(2,1)S(1)}, u32[]{:S(2)}, u32[]{:S(2)}) collective-permute-start(bf16[8,256,256]{2,1,0:T(8,128)(2,1)} %get-tuple-element.44), channel_id=1, source_target_pairs={{0,2},{2,0},{4,6},{6,4},{8,10},{10,8},{12,14},{14,12},{16,18},{18,... | collective-permute-start | bytes 3145736 | tf_op jit(solution)/shard_map/ppermute | solution.py:324
  140.0 1.3 copy-start.1
  142.8 1.0 copy-start.2
  143.8 29.3 %collective-permute-start.8 = (bf16[4,256,256]{2,1,0:T(8,128)(2,1)}, bf16[4,256,256]{2,1,0:T(8,128)(2,1)S(1)}, u32[]{:S(2)}, u32[]{:S(2)}) collective-permute-start(bf16[4,256,256]{2,1,0:T(8,128)(2,1)} %get-tuple-element.45.refs_8_), channel_id=1, source_target_pairs={{0,4},{2,6},{4,0},{6,2},{8,12},{10,14},{12,8},{14,10},{16,20},{18,... | collective-permute-start | bytes 1572872 | tf_op jit(solution)/shard_map/ppermute | solution.py:324
  173.1 8.0 %collective-permute-start.13 = (bf16[8,256,256]{2,1,0:T(8,128)(2,1)}, bf16[8,256,256]{2,1,0:T(8,128)(2,1)S(1)}, u32[]{:S(2)}, u32[]{:S(2)}) collective-permute-start(bf16[8,256,256]{2,1,0:T(8,128)(2,1)} %get-tuple-element.57), channel_id=1, source_target_pairs={{0,2},{2,0},{4,6},{6,4},{8,10},{10,8},{12,14},{14,12},{16,18},{18,... | collective-permute-start | bytes 3145736 | tf_op jit(solution)/shard_map/ppermute | solution.py:324
  173.2 1.2 copy-start.3
  174.4 0.9 copy-start.4
  176.3 4.8 %copy-start = (bf16[8,256,256]{2,1,0:T(8,128)(2,1)S(1)}, bf16[8,256,256]{2,1,0:T(8,128)(2,1)}, u32[]{:S(2)}) copy-start(bf16[8,256,256]{2,1,0:T(8,128)(2,1)} %get-tuple-element.56.refs_0_.refs_1_) | copy-start | bytes 3145732
  180.3 25.8 %collective-permute-start.9 = (bf16[128,4096]{1,0:T(8,128)(2,1)}, bf16[128,4096]{1,0:T(8,128)(2,1)}, u32[]{:S(2)}, u32[]{:S(2)}) collective-permute-start(bf16[128,4096]{1,0:T(8,128)(2,1)} %add_convert_fusion.1), channel_id=1, source_target_pairs={{0,1},{1,0},{2,3},{3,2},{4,5},{5,4},{6,7},{7,6},{8,9},{9,8},{10,11... | collective-permute-start | bytes 3145736 | tf_op jit(solution)/shard_map/ppermute | solution.py:459
  181.4 21.1 %copy-start.6 = (f32[256,256]{1,0:T(8,128)S(1)}, f32[256,256]{1,0:T(8,128)}, u32[]{:S(2)}) copy-start(f32[256,256]{1,0:T(8,128)} %get-tuple-element.52.refs_0_) | copy-start | bytes 786436
  181.4 14.2 %collective-permute-start.14 = (bf16[4,256,256]{2,1,0:T(8,128)(2,1)S(1)}, bf16[4,256,256]{2,1,0:T(8,128)(2,1)S(1)}, u32[]{:S(2)}, u32[]{:S(2)}) collective-permute-start(bf16[4,256,256]{2,1,0:T(8,128)(2,1)S(1)} %get-tuple-element.59.refs_2_), channel_id=1, source_target_pairs={{0,4},{2,6},{4,0},{6,2},{8,12},{10,14},{12,8},{14,10},{16,20},{18,... | collective-permute-start | bytes 1572872 | tf_op jit(solution)/shard_map/ppermute | solution.py:324
  182.0 14.1 %collective-permute-start.10 = (bf16[256,256]{1,0:T(8,128)(2,1)S(1)}, bf16[256,256]{1,0:T(8,128)(2,1)S(1)}, u32[]{:S(2)}, u32[]{:S(2)}) collective-permute-start(bf16[256,256]{1,0:T(8,128)(2,1)S(1)} %get-tuple-element.49.refs_4_), channel_id=1, source_target_pairs={{0,8},{2,10},{4,12},{6,14},{8,0},{10,2},{12,4},{14,6},{16,24},{18,... | collective-permute-start | bytes 393224 | tf_op jit(solution)/shard_map/ppermute | solution.py:324
  182.2 18.2 %collective-permute-start.11 = (bf16[256,256]{1,0:T(8,128)(2,1)}, bf16[256,256]{1,0:T(8,128)(2,1)S(1)}, u32[]{:S(2)}, u32[]{:S(2)}) collective-permute-start(bf16[256,256]{1,0:T(8,128)(2,1)} %get-tuple-element.54), channel_id=1, source_target_pairs={{0,16},{2,18},{4,20},{6,22},{8,24},{10,26},{12,28},{14,30},{16,0},... | collective-permute-start | bytes 393224 | tf_op jit(solution)/shard_map/ppermute | solution.py:324
  186.0 16.4 %collective-permute-start.12 = (bf16[256,256]{1,0:T(8,128)(2,1)}, bf16[256,256]{1,0:T(8,128)(2,1)S(1)}, u32[]{:S(2)}, u32[]{:S(2)}) collective-permute-start(bf16[256,256]{1,0:T(8,128)(2,1)} %get-tuple-element.55), channel_id=1, source_target_pairs={{0,24},{2,26},{4,28},{6,30},{8,16},{10,18},{12,20},{14,22},{16,8},... | collective-permute-start | bytes 393224 | tf_op jit(solution)/shard_map/ppermute | solution.py:324
  195.8 13.5 %collective-permute-start.15 = (bf16[256,256]{1,0:T(8,128)(2,1)S(1)}, bf16[256,256]{1,0:T(8,128)(2,1)S(1)}, u32[]{:S(2)}, u32[]{:S(2)}) collective-permute-start(bf16[256,256]{1,0:T(8,128)(2,1)S(1)} %get-tuple-element.60.refs_5_), channel_id=1, source_target_pairs={{0,8},{2,10},{4,12},{6,14},{8,0},{10,2},{12,4},{14,6},{16,24},{18,... | collective-permute-start | bytes 393224 | tf_op jit(solution)/shard_map/ppermute | solution.py:324
  196.0 14.8 %collective-permute-start.16 = (bf16[256,256]{1,0:T(8,128)(2,1)S(1)}, bf16[256,256]{1,0:T(8,128)(2,1)S(1)}, u32[]{:S(2)}, u32[]{:S(2)}) collective-permute-start(bf16[256,256]{1,0:T(8,128)(2,1)S(1)} %get-tuple-element.62), channel_id=1, source_target_pairs={{0,16},{2,18},{4,20},{6,22},{8,24},{10,26},{12,28},{14,30},{16,0},... | collective-permute-start | bytes 393224 | tf_op jit(solution)/shard_map/ppermute | solution.py:324
  200.4 10.5 %collective-permute-start.17 = (bf16[256,256]{1,0:T(8,128)(2,1)S(1)}, bf16[256,256]{1,0:T(8,128)(2,1)S(1)}, u32[]{:S(2)}, u32[]{:S(2)}) collective-permute-start(bf16[256,256]{1,0:T(8,128)(2,1)S(1)} %get-tuple-element.63), channel_id=1, source_target_pairs={{0,24},{2,26},{4,28},{6,30},{8,16},{10,18},{12,20},{14,22},{16,8},... | collective-permute-start | bytes 393224 | tf_op jit(solution)/shard_map/ppermute | solution.py:324
  202.5 8.3 %copy-start.5 = (f32[256,256]{1,0:T(8,128)S(1)}, f32[256,256]{1,0:T(8,128)}, u32[]{:S(2)}) copy-start(f32[256,256]{1,0:T(8,128)} %get-tuple-element.48.refs_2_.refs_0_) | copy-start | bytes 786436
  202.6 8.4 %copy-start.10 = (f32[256,256]{1,0:T(8,128)S(1)}, f32[256,256]{1,0:T(8,128)}, u32[]{:S(2)}) copy-start(f32[256,256]{1,0:T(8,128)} %get-tuple-element.37.refs_9_) | copy-start | bytes 786436
  202.6 8.4 %copy-start.11 = (f32[256,256]{1,0:T(8,128)S(1)}, f32[256,256]{1,0:T(8,128)}, u32[]{:S(2)}) copy-start(f32[256,256]{1,0:T(8,128)} %get-tuple-element.40.refs_8_) | copy-start | bytes 786436
Sparse Core Ops, SparseCore 0:
  10.3 69.4 all-gather.2
  108.6 87.9 reduce-scatter.1
